TPU v7x, 32 devices: a whole 2x2x4 slice. The times are simulated.
32 devices in a mesh: seg: 8 (over y, x, core), fft: 4 (over z).
Axes of the slice: x: 2, y: 2, z: 4, core: 2. Of those that a mesh axis runs over, the one named last changes fastest.
Arguments:
- voltage: float32 [8, 2, 256, 4096], P('seg', None, None, 'fft'), may hold values from -6 to 6
- chirp_phase: float32 [2, 512, 4096], P(None, 'fft'), may hold values from -3.140625 to 3.140625
Outputs:
- dedispersed: float32 [8, 2, 256, 4096], P('seg', None, None, 'fft')
All inputs are finite; a program needn't handle non-finite values.
Results may differ from a plain program's by a relative error of at most 0.0001.
Values sent between devices are 32-bit elements; how exact they have to be, the bound alone decides.
No kernel may reach another device: no remote copies, remote signals or barrier semaphores. Data moves between devices by JAX's collectives and lax.ppermute only.
A program may use at most 128 MiB of HBM per device.

v0:
```python
import math

import jax
import jax.numpy as jnp
import ml_dtypes
import numpy as np
from jax import lax
from jax.experimental import pallas as pl
from jax.experimental.pallas import tpu as pltpu
from jax.sharding import PartitionSpec as P

LANES = 128
SUB = 8
VMEM = 50 * 1024 * 1024


def turn(products, period):
    angles = np.mod(products, period).astype(np.float64) * (-2.0 * math.pi / period)
    return np.cos(angles), np.sin(angles)


def halves(table):
    high = table.astype(ml_dtypes.bfloat16)
    low = (table - high.astype(np.float64)).astype(ml_dtypes.bfloat16)
    return high, low


def split(values):
    high = values.astype(jnp.bfloat16)
    low = (values - high.astype(jnp.float32)).astype(jnp.bfloat16)
    return high, low


def thrice(values, axis):
    high, low = split(values)
    return jnp.concatenate([high, low, high] if axis == 0 else [high, high, low], axis=axis)


def right_table(table):
    high, low = halves(table)
    return np.concatenate([high, low, high], axis=-2)


def left_table(table):
    high, low = halves(table)
    return np.concatenate([high, high, low], axis=-1)


def dot(left, right):
    return jnp.dot(left, right, preferred_element_type=jnp.float32)


def scale_by(value, cos, sin):
    re, im = value
    near = 1e-12
    if abs(sin) < near:
        return value if cos > 0 else (-re, -im)
    if abs(cos) < near:
        return (-im, re) if sin > 0 else (im, -re)
    if abs(abs(cos) - abs(sin)) < near:
        size = abs(cos)
        first = re if cos > 0 else -re
        second = im if cos > 0 else -im
        third = im if sin > 0 else -im
        fourth = re if sin > 0 else -re
        return (first - third) * size, (second + fourth) * size
    return re * cos - im * sin, re * sin + im * cos


def plus(left, right):
    return left[0] + right[0], left[1] + right[1]


def minus(left, right):
    return left[0] - right[0], left[1] - right[1]


def small_dft(values, sign):
    count = len(values)
    if count == 1:
        return values
    if count == 2:
        return [plus(values[0], values[1]), minus(values[0], values[1])]
    if count == 4:
        even_sum, even_gap = plus(values[0], values[2]), minus(values[0], values[2])
        odd_sum, odd_gap = plus(values[1], values[3]), minus(values[1], values[3])
        turned = scale_by(odd_gap, 0.0, float(sign))
        return [plus(even_sum, odd_sum), plus(even_gap, turned), minus(even_sum, odd_sum), minus(even_gap, turned)]
    radix = 4 if count == 32 else 2
    part = count // radix
    pieces = [small_dft(values[i::radix], sign) for i in range(radix)]
    result = [None] * count
    for k in range(part):
        column = []
        for i in range(radix):
            angle = sign * 2.0 * math.pi * i * k / count
            column.append(scale_by(pieces[i][k], math.cos(angle), math.sin(angle)))
        for q, value in enumerate(small_dft(column, sign)):
            result[k + part * q] = value
    return result


def forward(value_at, twist, tables, grid):
    spectra = []
    for parity in range(2):
        values = [value_at(parity, j) for j in range(twist.shape[2])]
        for k, (re, im) in enumerate(small_dft(values, -1)):
            w_re, w_im = twist[parity, 0, pl.ds(k, 1)], twist[parity, 1, pl.ds(k, 1)]
            grid[parity, pl.ds(k * SUB, SUB), pl.ds(0, LANES)] = re * w_re - im * w_im
            grid[parity, pl.ds(k * SUB, SUB), pl.ds(LANES, LANES)] = re * w_im + im * w_re
        spectra.append(dot(thrice(grid[parity], 1), tables[parity]))
    even, odd = spectra
    return even + odd, even - odd


def backward(side, parity, twist, table, grid, put):
    grid[parity] = dot(thrice(side, 1), table)
    values = []
    for k in range(twist.shape[2]):
        re = grid[parity, pl.ds(k * SUB, SUB), pl.ds(0, LANES)]
        im = grid[parity, pl.ds(k * SUB, SUB), pl.ds(LANES, LANES)]
        w_re, w_im = twist[parity, 0, pl.ds(k, 1)], twist[parity, 1, pl.ds(k, 1)]
        values.append((re * w_re + im * w_im, im * w_re - re * w_im))
    for j, (re, im) in enumerate(small_dft(values, 1)):
        put(j, re, im)


def turned_by(angles):
    half = angles * 0.5
    square = half * half
    sin, cos = 0.0, 0.0
    for n in range(6, -1, -1):
        sin = sin * square + (-1.0) ** n / math.factorial(2 * n + 1)
        cos = cos * square + (-1.0) ** n / math.factorial(2 * n)
    sin = sin * half
    return 1.0 - 2.0 * sin * sin, 2.0 * sin * cos


def spread_kernel(x, table, turns, phases, out):
    count, slots, width = out.shape[0], out.shape[3], out.shape[4]
    sums = dot(table[...], thrice(jnp.concatenate([x[0, 0], x[0, 1]], axis=1), 0))
    sums = sums.reshape(count, 2, slots, 2 * width)
    turn_re, turn_im = turns[:, 0], turns[:, 1]
    for parity in range(2):
        lanes = slice(parity * width, (parity + 1) * width)
        ph_re, ph_im = phases[:, 2 * parity], phases[:, 2 * parity + 1]
        re, im = sums[:, 0, :, lanes], sums[:, 1, :, lanes]
        w_re = turn_re * ph_re - turn_im * ph_im
        w_im = turn_re * ph_im + turn_im * ph_re
        out[:, parity, 0] = re * w_re - im * w_im
        out[:, parity, 1] = re * w_im + im * w_re


def digits_swapped(tiles):
    lane = lax.broadcasted_iota(jnp.int32, tiles[0].shape, 1)
    step = 1
    while step < len(tiles):
        low_half = jnp.bitwise_and(lane, step) == 0
        swapped = list(tiles)
        for k in range(len(tiles)):
            if k & step == 0:
                first, second = tiles[k], tiles[k + step]
                swapped[k] = jnp.where(low_half, first, pltpu.roll(second, step, 1))
                swapped[k + step] = jnp.where(low_half, pltpu.roll(first, LANES - step, 1), second)
        tiles = swapped
        step *= 2
    return tiles


def chirp_kernel(place, angles, twist, tables, mirror, extra_turn, out, sides, grid, held):
    first_rows = jnp.logical_and(place[0] == 0, pl.program_id(0) == 0)
    points = twist.shape[2]
    for side in range(2):
        tiles = [angles[side, :, pl.ds(k * LANES, LANES)] for k in range(points)]
        for k, value in enumerate(digits_swapped(tiles)):
            cos, sin = turned_by(value)
            sides[side, pl.ds(k * SUB, SUB), pl.ds(0, LANES)] = cos
            sides[side, pl.ds(k * SUB, SUB), pl.ds(LANES, LANES)] = sin

    @pl.when(first_rows)
    def _():
        slot = lax.broadcasted_iota(jnp.int32, (SUB, LANES), 0)
        lane = lax.broadcasted_iota(jnp.int32, (SUB, LANES), 1)
        alive = jnp.logical_or(slot > 0, lane > 0)
        for part in range(2):
            lanes = pl.ds(part * LANES, LANES)
            sides[0, pl.ds(0, SUB), lanes] = jnp.where(alive, sides[0, pl.ds(0, SUB), lanes], 0.0)

    for parity in range(2):
        sign = 1.0 - 2.0 * parity
        for side in range(2):

            def put(j, re, im, parity=parity, side=side, sign=sign):
                held[parity, side, 0, j] = re
                held[parity, side, 1, j] = im
                if side == 1:
                    m_re, m_im = mirror[parity, 0, pl.ds(j, 1)], mirror[parity, 1, pl.ds(j, 1)]
                    out[j, parity, 0] = held[parity, 0, 0, j] + sign * (re * m_re + im * m_im)
                    out[j, parity, 1] = held[parity, 0, 1, j] + sign * (re * m_im - im * m_re)

            backward(sides[side], parity, twist, tables[parity], grid.at[side], put)

    @pl.when(first_rows)
    def _():
        keep = lax.broadcasted_iota(jnp.int32, (SUB, LANES), 0) > 0
        for parity in range(2):
            for j in range(points):
                w_re, w_im = extra_turn[parity, 0, pl.ds(j, 1)], extra_turn[parity, 1, pl.ds(j, 1)]
                near = 2.0 * held[parity, 0, 0, j]
                far = 2.0 * (held[parity, 1, 0, j] * w_re + held[parity, 1, 1, j] * w_im)
                out[j, parity, 0] = jnp.where(keep, out[j, parity, 0], near)
                out[j, parity, 1] = jnp.where(keep, out[j, parity, 1], far)


def response_kernel(parts, turns_in, phases_in, back_table, table, turns, phases, out, packed):
    sources, slots = parts.shape[0], parts.shape[3]
    count, out_slots = out.shape[0], out.shape[4]
    depth = 2 * sources * slots

    @pl.when(pl.program_id(0) == 0)
    def _():
        for source in range(sources):
            t_re, t_im = turns_in[source, 0], turns_in[source, 1]
            for parity in range(2):
                ph_re, ph_im = phases_in[source, 2 * parity], phases_in[source, 2 * parity + 1]
                w_re = t_re * ph_re - t_im * ph_im
                w_im = t_re * ph_im + t_im * ph_re
                re, im = parts[source, parity, 0], parts[source, parity, 1]
                lanes = pl.ds(parity * LANES, LANES)
                pair = jnp.concatenate([re * w_re + im * w_im, im * w_re - re * w_im], axis=0)
                high, low = split(pair)
                for n, value in enumerate((high, low, high)):
                    packed[pl.ds(n * depth + 2 * source * slots, 2 * slots), lanes] = value

    taps = dot(back_table[...], packed[...])
    sums = dot(table[...], thrice(taps, 0)).reshape(count, 2, out_slots, 2 * LANES)
    turn_re, turn_im = turns[:, 0], turns[:, 1]
    for parity in range(2):
        lanes = slice(parity * LANES, (parity + 1) * LANES)
        ph_re, ph_im = phases[:, 2 * parity], phases[:, 2 * parity + 1]
        re, im = sums[:, 0, :, lanes], sums[:, 1, :, lanes]
        w_re = turn_re * ph_re - turn_im * ph_im
        w_im = turn_re * ph_im + turn_im * ph_re
        out[:, 0, parity, 0] = re * w_re - im * w_im
        out[:, 0, parity, 1] = re * w_im + im * w_re


def forward_kernel(x, twist, tables, out, grid):
    tiles = x.shape[5] // LANES
    for n in range(x.shape[0]):

        def value_at(parity, j, n=n):
            group, tile = divmod(j, tiles)
            lanes = pl.ds(tile * LANES, LANES)
            return x[n, group, parity, 0, :, lanes], x[n, group, parity, 1, :, lanes]

        upper, lower = forward(value_at, twist, tables, grid.at[n])
        out[n, 0] = upper
        out[n, 1] = lower


def apply_kernel(taps, spectrum, twist, tables, out, raw, response, past, sides, grid):
    step = pl.program_id(0)
    points = twist.shape[2]
    tiles = out.shape[5] // LANES
    re_lanes, im_lanes = pl.ds(0, LANES), pl.ds(LANES, LANES)

    @pl.when(step == 0)
    def _():
        past[...] = jnp.zeros_like(past)

    @pl.when(step < 2)
    def _():
        for n in range(2):

            def value_at(parity, j, n=n):
                return taps[j, n, parity, 0], taps[j, n, parity, 1]

            upper, lower = forward(value_at, twist, tables, grid.at[n])
            raw[2 * step + n, 0] = upper
            raw[2 * step + n, 1] = lower

    @pl.when(step == 1)
    def _():
        sign = 1.0 - 2.0 * (lax.broadcasted_iota(jnp.int32, (SUB, LANES), 0) % 2).astype(jnp.float32)
        for side in range(2):
            for k in range(points):
                rows = pl.ds(k * SUB, SUB)
                res = [raw[j, side, rows, re_lanes] for j in range(4)]
                ims = [raw[j, side, rows, im_lanes] for j in range(4)]
                for j in range(4):
                    response[j, side, rows, re_lanes] = res[j] - sign * ims[j - 1]
                    response[j, side, rows, im_lanes] = ims[j] + sign * res[j - 1]

    @pl.when(step >= 2)
    def _():
        window = [past.at[n] for n in range(3)] + [spectrum.at[n] for n in range(2)]
        for k in range(points):
            rows = pl.ds(k * SUB, SUB)
            sums = [[], []]
            for side in range(2):
                xs = [(ref[side, rows, re_lanes], ref[side, rows, im_lanes]) for ref in window]
                totals = [None, None]
                for j in range(4):
                    h_re, h_im = response[j, side, rows, re_lanes], response[j, side, rows, im_lanes]
                    for n in range(2):
                        x_re, x_im = xs[3 + n - j]
                        term = h_re * x_re - h_im * x_im, h_re * x_im + h_im * x_re
                        totals[n] = term if j == 0 else plus(totals[n], term)
                for n in range(2):
                    sums[n].append(totals[n])
            for n in range(2):
                for parity, value in enumerate((plus(*sums[n]), minus(*sums[n]))):
                    sides[n, parity, rows, re_lanes] = value[0]
                    sides[n, parity, rows, im_lanes] = value[1]
        for n in range(2):
            for parity in range(2):

                def put(j, re, im, n=n, parity=parity):
                    group, tile = divmod(j, tiles)
                    lanes = pl.ds(tile * LANES, LANES)
                    out[n, group, parity, 0, :, lanes] = re
                    out[n, group, parity, 1, :, lanes] = im

                backward(sides[n, parity], parity, twist, tables[2 + parity], grid.at[n], put)
        past[0] = past[2]
        past[1] = spectrum[0]
        past[2] = spectrum[1]


def gather_kernel(parts, turns, phases, table, out):
    count, slots, width = parts.shape[0], parts.shape[3], parts.shape[4]
    turn_re, turn_im = turns[:, 0], turns[:, 1]
    columns = []
    for parity in range(2):
        ph_re, ph_im = phases[:, 2 * parity], phases[:, 2 * parity + 1]
        w_re = turn_re * ph_re - turn_im * ph_im
        w_im = turn_re * ph_im + turn_im * ph_re
        re, im = parts[:, parity, 0], parts[:, parity, 1]
        pair = jnp.stack([re * w_re + im * w_im, im * w_re - re * w_im], axis=1)
        columns.append(pair.reshape(count * 2 * slots, width))
    sums = dot(table[...], thrice(jnp.concatenate(columns, axis=1), 0))
    for parity in range(2):
        out[0, parity] = sums[:, parity * width : (parity + 1) * width]


def whole(shape):
    return pl.BlockSpec(shape, lambda i, *_: (0,) * len(shape))


def call(kernel, name, grid, in_specs, out_specs, out_shape, scratch, flops, size, scalars=0):
    return pl.pallas_call(
        kernel,
        grid_spec=pltpu.PrefetchScalarGridSpec(
            num_scalar_prefetch=scalars,
            grid=(grid,),
            in_specs=in_specs,
            out_specs=out_specs,
            scratch_shapes=scratch,
        ),
        out_shape=jax.ShapeDtypeStruct(out_shape, jnp.float32),
        compiler_params=pltpu.CompilerParams(vmem_limit_bytes=VMEM, dimension_semantics=("arbitrary",)),
        cost_estimate=pl.CostEstimate(flops=int(flops), bytes_accessed=int(size), transcendentals=0),
        name=name,
    )


def exchange(values):
    return lax.all_to_all(values, ("seg", "fft"), split_axis=0, concat_axis=0, tiled=True)


def phase_pair(odd_rows, column, period):
    even = np.stack(turn(odd_rows * column, period), axis=-1)
    odd = np.stack(turn(odd_rows * (2 * column + 1), 2 * period), axis=-1)
    return np.concatenate([even, odd], axis=-1)


def per_device(voltage, chirp_phase):
    groups, segments = lax.axis_size("fft"), lax.axis_size("seg")
    group, segment = lax.axis_index("fft"), lax.axis_index("seg")
    count = groups * segments
    position = segment * groups + group
    quarter, width = voltage.shape[2], voltage.shape[3]
    row_count, half = 4 * quarter, 2 * quarter
    columns = width * groups
    points = columns // LANES
    total = row_count * columns
    short = total // 2
    slots = half // groups
    tile, narrow = min(2 * LANES, width // 4), LANES
    f32 = jnp.float32

    keys, lanes = np.arange(points), np.arange(LANES)
    twist = np.stack(
        [
            np.stack(turn(keys[:, None] * lanes[None, :], columns)),
            np.stack(turn(keys[:, None] * (2 * lanes[None, :] + 1), 2 * columns)),
        ]
    ).astype(np.float32)
    tables = []
    for cos, sin in (
        turn(lanes[:, None] * lanes[None, :], LANES),
        turn((2 * lanes[:, None] + 1) * lanes[None, :], 2 * LANES),
    ):
        tables.append(np.block([[cos, sin], [-sin, cos]]))
    column_tables = [twist, right_table(np.stack(tables + [table.T for table in tables]))]
    digit_order = (LANES // points * (lanes % points) + lanes // points).astype(np.int64)
    digit_order = np.concatenate([digit_order, LANES + digit_order])
    swapped_tables = right_table(np.stack([table.T[digit_order] for table in tables]))
    column_specs = [whole(table.shape) for table in column_tables]

    own_rows = max(SUB, quarter // count)
    odd_rows = 2 * np.arange(own_rows * count) + 1
    live = (odd_rows < 2 * quarter).astype(np.float64)
    cos, sin = turn(odd_rows[:, None] * np.arange(quarter)[None, :], 2 * half)
    row_table = np.stack([cos, sin], axis=1) * live[:, None, None]
    row_table = row_table.reshape(count, own_rows, 2, quarter).transpose(0, 2, 1, 3).reshape(-1, quarter)
    back_table = left_table(row_table.T / short)
    row_table = left_table(row_table)
    turns = np.stack(turn(odd_rows[:, None] * np.arange(width)[None, :], 2 * short))
    turns = turns.reshape(2, count, own_rows, width).transpose(1, 0, 2, 3).astype(np.float32)

    def row_phases(column_starts):
        table = phase_pair(odd_rows[None, :], column_starts[:, None], 2 * short)
        table = table.reshape(-1, count, own_rows, 4).transpose(0, 1, 3, 2)
        return jnp.asarray(table[..., None].astype(np.float32))

    phases = lax.dynamic_index_in_dim(row_phases(np.arange(groups) * width), group, 0, keepdims=False)

    chirp_slots = max(SUB, slots // segments)
    holders = slots // chirp_slots
    blocks = chirp_slots // SUB
    start = jnp.minimum(segment, holders - 1) * blocks
    place = jnp.stack([position, start]).astype(jnp.int32)
    every = LANES * keys[:, None] + lanes[None, :]
    extra_turn = np.stack(
        [np.stack(turn(half * every, total)), np.stack(turn(half * (2 * every + 1), 2 * total))]
    ).astype(np.float32)
    mirror = np.stack(
        [np.stack(turn(every, columns)), np.stack(turn((1 - columns) * (2 * every + 1), 2 * columns))]
    ).astype(np.float32)
    cells = (points * SUB, 2 * LANES)
    chirp_columns = call(
        chirp_kernel,
        "chirp_columns",
        blocks,
        [
            pl.BlockSpec((2, SUB, columns), lambda i, place: (0, place[1] + i, 0)),
            whole(twist.shape),
            whole(swapped_tables.shape),
            whole(mirror.shape),
            whole(extra_turn.shape),
        ],
        pl.BlockSpec((points, 2, 2, SUB, LANES), lambda i, place: (0, 0, 0, i, 0)),
        (points, 2, 2, chirp_slots, LANES),
        [
            pltpu.VMEM((2,) + cells, f32),
            pltpu.VMEM((2, 2) + cells, f32),
            pltpu.VMEM((2, 2, 2, points, SUB, LANES), f32),
        ],
        4e8 * blocks,
        3e6,
        scalars=1,
    )(place, chirp_phase, twist, swapped_tables, mirror, extra_turn)
    if holders < segments:
        chirp_columns = jnp.where(segment < holders, chirp_columns, 0.0)
    if count > points:
        chirp_columns = jnp.pad(chirp_columns, ((0, count - points),) + ((0, 0),) * 4)
    chirp_parts = exchange(chirp_columns)[: holders * groups]

    rows = np.arange(half)
    order = rows.reshape(groups, holders, chirp_slots).transpose(1, 0, 2)
    chirp_turns = np.stack(turn(order[..., None] * lanes, total), axis=2).astype(np.float32)
    block_of = np.arange(points)
    chirp_phases = phase_pair(order[None], LANES * block_of[:, None, None, None], total)
    chirp_phases = chirp_phases.reshape(points, holders * groups, chirp_slots, 4).transpose(0, 1, 3, 2)
    chirp_phases = jnp.asarray(chirp_phases[..., None].astype(np.float32))
    chirp_turns = chirp_turns.reshape(holders * groups, 2, chirp_slots, LANES)
    cos, sin = turn(rows[None, :] * np.arange(row_count)[:, None], row_count)
    cos[:, 0] = 0.5
    sin[:, 0] = np.where(np.arange(row_count) % 2 == 0, 0.5, -0.5)
    taps_table = np.stack([cos, sin], axis=1).reshape(row_count, 2, groups, holders, chirp_slots) / total
    taps_table = taps_table.transpose(0, 3, 2, 1, 4).reshape(row_count, 2 * half)
    taps_table = left_table(taps_table)
    own_block = jnp.minimum(position, points - 1)
    own_chirp_phases = lax.dynamic_index_in_dim(chirp_phases, own_block, 0, keepdims=False)
    own_row_phases = lax.dynamic_index_in_dim(row_phases(block_of * LANES), own_block, 0, keepdims=False)
    response_shape = (count, 4, 2, 2, own_rows, LANES)
    response = call(
        response_kernel,
        "response",
        4,
        [
            whole(chirp_parts.shape),
            whole(chirp_turns.shape),
            whole(own_chirp_phases.shape),
            pl.BlockSpec((quarter, taps_table.shape[1]), lambda i: (i, 0)),
            whole(row_table.shape),
            pl.BlockSpec((count, 2, own_rows, LANES), lambda i: (0, 0, 0, 0)),
            whole(own_row_phases.shape),
        ],
        pl.BlockSpec((count, 1, 2, 2, own_rows, LANES), lambda i: (0, i, 0, 0, 0, 0)),
        response_shape,
        [pltpu.VMEM((6 * half, 2 * LANES), jnp.bfloat16)],
        5e9,
        1e7,
    )(chirp_parts, chirp_turns, own_chirp_phases, taps_table, row_table, turns, own_row_phases)
    taps = exchange(response)[:points]

    spread_shape = (count, 2, 2, own_rows, width)
    spread = call(
        spread_kernel,
        "spread",
        width // tile,
        [
            pl.BlockSpec((1, 2, quarter, tile), lambda c: (0, 0, 0, c)),
            whole(row_table.shape),
            pl.BlockSpec((count, 2, own_rows, tile), lambda c: (0, 0, 0, c)),
            whole(phases.shape),
        ],
        pl.BlockSpec((count, 2, 2, own_rows, tile), lambda c: (0, 0, 0, 0, c)),
        spread_shape,
        [],
        2e9,
        1e7,
    )(voltage, row_table, turns, phases)
    spread = exchange(spread).reshape(segments, groups, 2, 2, own_rows, width)

    pair_scratch = pltpu.VMEM((2, 2) + cells, f32)
    spectrum = call(
        forward_kernel,
        "forward",
        segments // 2,
        [pl.BlockSpec((2, groups, 2, 2, own_rows, width), lambda s: (s, 0, 0, 0, 0, 0))] + column_specs,
        pl.BlockSpec((2, 2) + cells, lambda s: (s, 0, 0, 0)),
        (segments, 2) + cells,
        [pair_scratch],
        2e9,
        1e7,
    )(spread, *column_tables)

    def lagged(i):
        return jnp.maximum(i - 2, 0)

    packed = call(
        apply_kernel,
        "apply",
        segments // 2 + 2,
        [
            pl.BlockSpec((points, 2, 2, 2, own_rows, LANES), lambda i: (0, jnp.minimum(i, 1), 0, 0, 0, 0)),
            pl.BlockSpec((2, 2) + cells, lambda i: (lagged(i), 0, 0, 0)),
        ]
        + column_specs,
        pl.BlockSpec((2, groups, 2, 2, own_rows, width), lambda i: (lagged(i), 0, 0, 0, 0, 0)),
        (segments, groups, 2, 2, own_rows, width),
        [
            pltpu.VMEM((4, 2) + cells, f32),
            pltpu.VMEM((4, 2) + cells, f32),
            pltpu.VMEM((3, 2) + cells, f32),
            pair_scratch,
            pair_scratch,
        ],
        4e9,
        2e7,
    )(taps, spectrum, *column_tables)
    parts = exchange(packed.reshape(spread_shape))

    return call(
        gather_kernel,
        "gather",
        width // narrow,
        [
            pl.BlockSpec((count, 2, 2, own_rows, narrow), lambda c: (0, 0, 0, 0, c)),
            pl.BlockSpec((count, 2, own_rows, narrow), lambda c: (0, 0, 0, c)),
            whole(phases.shape),
            whole(back_table.shape),
        ],
        pl.BlockSpec((1, 2, quarter, narrow), lambda c: (0, 0, 0, c)),
        (1, 2, quarter, width),
        [],
        2e9,
        1e7,
    )(parts, turns, phases, back_table)


def solution(mesh):
    in_specs = (P("seg", None, None, "fft"), P(None, "fft", None))
    out_specs = P("seg", None, None, "fft")
    return jax.shard_map(per_device, mesh=mesh, in_specs=in_specs, out_specs=out_specs, check_vma=False)
```

profile of v0, /device:TPU:1, one launch (start us, length us, event | category | flops | bytes accessed | tf_op | source)
XLA Modules:
  0.0 310.2 jit_solution(16734862810991119545)
XLA Ops:
  0.0 0.1 pad_add_fusion.place
  0.1 1.1 copy-done.6
  1.2 0.8 copy-done.7
  2.1 0.8 copy-done.9
  2.9 0.8 copy-done.10
  3.7 6.1 %chirp_columns.1 = f32[32,2,2,16,128]{4,3,2,1,0:T(8,128)} custom-call(s32[2]{0:T(128)S(1)} %pad_add_fusion.place, f32[2,128,4096]{2,1,0:T(8,128)} %angles.1, f32[2,2,32,128]{3,2,1,0:T(8,128)S(1)} %copy-done.7, bf16[2,768,256]{2,1,0:T(8,128)(2,1)S(1)} %copy-done.6, f32[2,2,32,128]{3,2,1,0:T(8,128)S(1)} %copy-done.10, f32[2,2,32,128]{3,2,1,0:T(8,128)S(1)} %copy-done.9), custom_call_target="tpu_custom_call" | custom-call | flops 800000000 | bytes 3000000 | tf_op jit(solution)/shard_map/chirp_columns/pallas_call | solution.py:443
  9.8 7.2 %all-to-all-start = ((f32[32,2,2,16,128]{4,3,2,1,0:T(8,128)}), f32[32,2,2,16,128]{4,3,2,1,0:T(8,128)}, u32[]{:S(2)}, u32[]{:S(2)}) async-start(f32[32,2,2,16,128]{4,3,2,1,0:T(8,128)} %chirp_columns.1), calls=%async_computation | async-start | bytes 2097152 | tf_op jit(solution)/shard_map/all_to_all | solution.py:369
  17.0 0.7 dynamic-slice_bitcast_fusion.1
  17.7 0.5 copy.18.phases
  18.2 0.0 copy-done.1
  18.2 0.0 copy-done.5
  18.2 5.5 %spread.1 = f32[32,2,2,8,1024]{4,3,2,1,0:T(8,128)} custom-call(f32[1,2,256,1024]{3,2,1,0:T(8,128)S(1)} %copy-done.1, bf16[512,768]{1,0:T(8,128)(2,1)S(1)} %copy-done.5, f32[32,2,8,1024]{3,2,1,0:T(8,128)} %constant.67.clone.turns, f32[32,4,8,1]{3,2,1,0:T(8,128)S(1)} %copy.18.phases), custom_call_target="tpu_custom_call" | custom-call | flops 2000000000 | bytes 10000000 | tf_op jit(solution)/shard_map/spread/pallas_call | solution.py:511
  23.7 19.6 %all-to-all-done.parts = f32[32,2,2,16,128]{4,3,2,1,0:T(8,128)} async-done(((f32[32,2,2,16,128]{4,3,2,1,0:T(8,128)}), f32[32,2,2,16,128]{4,3,2,1,0:T(8,128)}, u32[]{:S(2)}, u32[]{:S(2)}) %all-to-all-start) | async-done | bytes 1048608 | tf_op jit(solution)/shard_map/all_to_all | solution.py:369
  43.4 3.3 %all-to-all-start.2 = ((f32[32,2,2,8,1024]{4,3,2,1,0:T(8,128)}), f32[32,2,2,8,1024]{4,3,2,1,0:T(8,128)}, u32[]{:S(2)}, u32[]{:S(2)}) async-start(f32[32,2,2,8,1024]{4,3,2,1,0:T(8,128)} %spread.1), calls=%async_computation.2 | async-start | bytes 8388608 | tf_op jit(solution)/shard_map/all_to_all | solution.py:369
  46.7 0.7 dynamic-slice_bitcast_fusion.2
  47.4 0.5 copy.17.phases
  48.0 0.8 dynamic-slice_bitcast_fusion
  48.7 1.0 copy.16.phases_in
  49.7 0.0 copy-done.11
  49.7 8.6 %response.1 = f32[32,4,2,2,8,128]{5,4,3,2,1,0:T(8,128)} custom-call(f32[32,2,2,16,128]{4,3,2,1,0:T(8,128)} %all-to-all-done.parts, f32[32,2,16,128]{3,2,1,0:T(8,128)S(1)} %copy-done.11, f32[32,4,16,1]{3,2,1,0:T(8,128)S(1)} %copy.16.phases_in, bf16[1024,3072]{1,0:T(8,128)(2,1)} %constant.65.clone.back_table, bf16[512,768]{1,0:T(8,128)(2,1)S(1)} %copy-done.5, ...), custom_call_target="tpu_custom_call" | custom-call | flops 5000000000 | bytes 10000000 | tf_op jit(solution)/shard_map/response/pallas_call | solution.py:489
  58.3 80.2 %all-to-all-done.2 = f32[32,2,2,8,1024]{4,3,2,1,0:T(8,128)} async-done(((f32[32,2,2,8,1024]{4,3,2,1,0:T(8,128)}), f32[32,2,2,8,1024]{4,3,2,1,0:T(8,128)}, u32[]{:S(2)}, u32[]{:S(2)}) %all-to-all-start.2) | async-done | bytes 4194336 | tf_op jit(solution)/shard_map/all_to_all | solution.py:369
  138.5 5.9 %all-to-all-start.1 = ((f32[32,4,2,2,8,128]{5,4,3,2,1,0:T(8,128)}), f32[32,4,2,2,8,128]{5,4,3,2,1,0:T(8,128)S(1)}, u32[]{:S(2)}, u32[]{:S(2)}) async-start(f32[32,4,2,2,8,128]{5,4,3,2,1,0:T(8,128)} %response.1), calls=%async_computation.1 | async-start | bytes 4194304 | tf_op jit(solution)/shard_map/all_to_all | solution.py:369
  144.5 0.0 copy-done.8
  144.5 0.0 copy-start.2
  144.5 1.4 copy-done.2
  145.9 6.7 %forward.1.spectrum = f32[8,2,256,256]{3,2,1,0:T(8,128)} custom-call(f32[8,4,2,2,8,1024]{5,4,3,2,1,0:T(8,128)} %bitcast.5.x, f32[2,2,32,128]{3,2,1,0:T(8,128)S(1)} %copy-done.8, bf16[4,768,256]{2,1,0:T(8,128)(2,1)S(1)} %copy-done.2), custom_call_target="tpu_custom_call" | custom-call | flops 2000000000 | bytes 10000000 | tf_op jit(solution)/shard_map/forward/pallas_call | solution.py:530
  152.5 40.2 %all-to-all-done.1.taps = f32[32,4,2,2,8,128]{5,4,3,2,1,0:T(8,128)S(1)} async-done(((f32[32,4,2,2,8,128]{5,4,3,2,1,0:T(8,128)}), f32[32,4,2,2,8,128]{5,4,3,2,1,0:T(8,128)S(1)}, u32[]{:S(2)}, u32[]{:S(2)}) %all-to-all-start.1) | async-done | bytes 2097184 | tf_op jit(solution)/shard_map/all_to_all | solution.py:369
  192.7 1.4 copy-done.3
  194.1 10.7 %apply.1 = f32[8,4,2,2,8,1024]{5,4,3,2,1,0:T(8,128)} custom-call(f32[32,4,2,2,8,128]{5,4,3,2,1,0:T(8,128)S(1)} %all-to-all-done.1.taps, f32[8,2,256,256]{3,2,1,0:T(8,128)} %forward.1.spectrum, f32[2,2,32,128]{3,2,1,0:T(8,128)S(1)} %copy-done.8, bf16[4,768,256]{2,1,0:T(8,128)(2,1)S(1)} %copy-done.3), custom_call_target="tpu_custom_call" | custom-call | flops 4000000000 | bytes 20000000 | tf_op jit(solution)/shard_map/apply/pallas_call | solution.py:545
  204.8 97.3 %all_to_all.20.parts = f32[32,2,2,8,1024]{4,3,2,1,0:T(8,128)} all-to-all(f32[32,2,2,8,1024]{4,3,2,1,0:T(8,128)} %bitcast.10), channel_id=1, replica_groups=mesh['seg'=8,'fft'=4] {'seg','fft'}, dimensions={0} | all-to-all | bytes 8388608 | tf_op jit(solution)/shard_map/all_to_all | solution.py:369
  302.1 0.0 copy-done
  302.1 8.1 %gather.1 = f32[1,2,256,1024]{3,2,1,0:T(8,128)} custom-call(f32[32,2,2,8,1024]{4,3,2,1,0:T(8,128)} %all_to_all.20.parts, f32[32,2,8,1024]{3,2,1,0:T(8,128)S(1)} %copy-done, f32[32,4,8,1]{3,2,1,0:T(8,128)S(1)} %copy.18.phases, bf16[256,1536]{1,0:T(8,128)(2,1)S(1)} %copy-done.4), custom_call_target="tpu_custom_call" | custom-call | flops 2000000000 | bytes 10000000 | tf_op jit(solution)/shard_map/gather/pallas_call | solution.py:568
  (12 shorter events, 0.0 us)
Async XLA Ops:
  0.1 1.1 copy-start.6
  1.2 0.8 copy-start.7
  2.0 0.8 copy-start.9
  2.9 0.8 copy-start.10
  3.7 14.5 %copy-start.1 = (f32[1,2,256,1024]{3,2,1,0:T(8,128)S(1)}, f32[1,2,256,1024]{3,2,1,0:T(8,128)}, u32[]{:S(2)}) copy-start(f32[1,2,256,1024]{3,2,1,0:T(8,128)} %x.1) | copy-start | bytes 6291460
  3.7 14.5 %copy-start.5 = (bf16[512,768]{1,0:T(8,128)(2,1)S(1)}, bf16[512,768]{1,0:T(8,128)(2,1)}, u32[]{:S(2)}) copy-start(bf16[512,768]{1,0:T(8,128)(2,1)} %constant.66.clone.table) | copy-start | bytes 2359300
  9.8 33.6 %all-to-all-start = ((f32[32,2,2,16,128]{4,3,2,1,0:T(8,128)}), f32[32,2,2,16,128]{4,3,2,1,0:T(8,128)}, u32[]{:S(2)}, u32[]{:S(2)}) async-start(f32[32,2,2,16,128]{4,3,2,1,0:T(8,128)} %chirp_columns.1), calls=%async_computation | async-start | bytes 2097152 | tf_op jit(solution)/shard_map/all_to_all | solution.py:369
  23.7 26.0 %copy-start.11 = (f32[32,2,16,128]{3,2,1,0:T(8,128)S(1)}, f32[32,2,16,128]{3,2,1,0:T(8,128)}, u32[]{:S(2)}) copy-start(f32[32,2,16,128]{3,2,1,0:T(8,128)} %constant.64.clone.turns_in) | copy-start | bytes 1572868
  43.4 95.2 %all-to-all-start.2 = ((f32[32,2,2,8,1024]{4,3,2,1,0:T(8,128)}), f32[32,2,2,8,1024]{4,3,2,1,0:T(8,128)}, u32[]{:S(2)}, u32[]{:S(2)}) async-start(f32[32,2,2,8,1024]{4,3,2,1,0:T(8,128)} %spread.1), calls=%async_computation.2 | async-start | bytes 8388608 | tf_op jit(solution)/shard_map/all_to_all | solution.py:369
  58.3 86.1 %copy-start.8 = (f32[2,2,32,128]{3,2,1,0:T(8,128)S(1)}, f32[2,2,32,128]{3,2,1,0:T(8,128)}, u32[]{:S(2)}) copy-start(f32[2,2,32,128]{3,2,1,0:T(8,128)} %constant.58.clone.twist) | copy-start | bytes 196612
  138.5 54.2 %all-to-all-start.1 = ((f32[32,4,2,2,8,128]{5,4,3,2,1,0:T(8,128)}), f32[32,4,2,2,8,128]{5,4,3,2,1,0:T(8,128)S(1)}, u32[]{:S(2)}, u32[]{:S(2)}) async-start(f32[32,4,2,2,8,128]{5,4,3,2,1,0:T(8,128)} %response.1), calls=%async_computation.1 | async-start | bytes 4194304 | tf_op jit(solution)/shard_map/all_to_all | solution.py:369
  144.5 1.4 copy-start.2
  192.7 1.4 copy-start.3
  204.8 97.3 %copy-start = (f32[32,2,8,1024]{3,2,1,0:T(8,128)S(1)}, f32[32,2,8,1024]{3,2,1,0:T(8,128)}, u32[]{:S(2)}) copy-start(f32[32,2,8,1024]{3,2,1,0:T(8,128)} %constant.67.clone.turns) | copy-start | bytes 6291460
  204.8 97.3 %copy-start.4 = (bf16[256,1536]{1,0:T(8,128)(2,1)S(1)}, bf16[256,1536]{1,0:T(8,128)(2,1)}, u32[]{:S(2)}) copy-start(bf16[256,1536]{1,0:T(8,128)(2,1)} %constant.69.clone.table) | copy-start | bytes 2359300
where the time goes:
time: 311 us; the launch traced here: 310 us
  waiting for transfers between devices  140 us (45%)
  blocking collectives  97.3 us (31%)
  Pallas kernels  45.6 us (15%)
  starting transfers between devices  16.4 us (5%)
  local copies, waits for them, and re-layouts  10.8 us (3%)
    all_to_all x3, waiting for transfers between devices, exchange(): lax.all_to_all(values, ('seg', 'fft'), split_axis=0, concat_axis=0, tiled...  140 us
    all_to_all x1, blocking collectives, exchange(): lax.all_to_all(values, ('seg', 'fft'), split_axis=0, concat_axis=0, tiled...  97.3 us
    all_to_all x3, starting transfers between devices, exchange(): lax.all_to_all(values, ('seg', 'fft'), split_axis=0, concat_axis=0, tiled...  16.4 us
    pallas_call x1, Pallas kernels, per_device(): call(apply_kernel, 'apply', segments // 2 + 2, [pl.BlockSpec((points, 2,...  10.7 us
    pallas_call x1, Pallas kernels, per_device(): call(response_kernel, 'response', 4, [whole(chirp_parts.shape), whole(chi...  8.58 us
    pallas_call x1, Pallas kernels, per_device(): call(gather_kernel, 'gather', width // narrow, [pl.BlockSpec((count, 2, 2...  8.12 us
    pallas_call x1, Pallas kernels, per_device(): call(forward_kernel, 'forward', segments // 2, [pl.BlockSpec((2, groups,...  6.66 us
    unnamed x24, local copies, waits for them, and re-layouts  6.48 us
  transfers between devices with their start and end apart: 3, of which 3 were waited for; matrix products, arithmetic and copies ran while one was open for 1% of the time, Pallas kernels for 7%

commit v1 on v0

--- a/solution.py
+++ b/solution.py
@@ -167,49 +167,55 @@
     return tiles
 
 
-def chirp_kernel(place, angles, twist, tables, mirror, extra_turn, out, sides, grid, held):
-    first_rows = jnp.logical_and(place[0] == 0, pl.program_id(0) == 0)
-    points = twist.shape[2]
-    for side in range(2):
-        tiles = [angles[side, :, pl.ds(k * LANES, LANES)] for k in range(points)]
-        for k, value in enumerate(digits_swapped(tiles)):
-            cos, sin = turned_by(value)
-            sides[side, pl.ds(k * SUB, SUB), pl.ds(0, LANES)] = cos
-            sides[side, pl.ds(k * SUB, SUB), pl.ds(LANES, LANES)] = sin
-
-    @pl.when(first_rows)
+def chirp_kernel(place, angles, small, tables, out, sides, grid, held):
+    twist, mirror, extra_turn = (small.at[n] for n in range(3))
+    points = small.shape[3]
+    blocks = angles.shape[1] // SUB
+    for block in range(blocks):
+        for side in range(2):
+            rows = pl.ds(block * SUB, SUB)
+            tiles = [angles[side, rows, pl.ds(k * LANES, LANES)] for k in range(points)]
+            for k, value in enumerate(digits_swapped(tiles)):
+                cos, sin = turned_by(value)
+                sides[block, side, pl.ds(k * SUB, SUB), pl.ds(0, LANES)] = cos
+                sides[block, side, pl.ds(k * SUB, SUB), pl.ds(LANES, LANES)] = sin
+
+    @pl.when(place[0] == 0)
     def _():
         slot = lax.broadcasted_iota(jnp.int32, (SUB, LANES), 0)
         lane = lax.broadcasted_iota(jnp.int32, (SUB, LANES), 1)
         alive = jnp.logical_or(slot > 0, lane > 0)
         for part in range(2):
             lanes = pl.ds(part * LANES, LANES)
-            sides[0, pl.ds(0, SUB), lanes] = jnp.where(alive, sides[0, pl.ds(0, SUB), lanes], 0.0)
-
-    for parity in range(2):
-        sign = 1.0 - 2.0 * parity
-        for side in range(2):
-
-            def put(j, re, im, parity=parity, side=side, sign=sign):
-                held[parity, side, 0, j] = re
-                held[parity, side, 1, j] = im
-                if side == 1:
-                    m_re, m_im = mirror[parity, 0, pl.ds(j, 1)], mirror[parity, 1, pl.ds(j, 1)]
-                    out[j, parity, 0] = held[parity, 0, 0, j] + sign * (re * m_re + im * m_im)
-                    out[j, parity, 1] = held[parity, 0, 1, j] + sign * (re * m_im - im * m_re)
-
-            backward(sides[side], parity, twist, tables[parity], grid.at[side], put)
-
-    @pl.when(first_rows)
+            sides[0, 0, pl.ds(0, SUB), lanes] = jnp.where(alive, sides[0, 0, pl.ds(0, SUB), lanes], 0.0)
+
+    for block in range(blocks):
+        rows = pl.ds(block * SUB, SUB)
+        for parity in range(2):
+            for side in range(2):
+
+                def put(j, re, im, block=block, rows=rows, parity=parity, side=side):
+                    held[block, parity, side, 0, j] = re
+                    held[block, parity, side, 1, j] = im
+                    if side == 1:
+                        sign = 1.0 - 2.0 * parity
+                        m_re, m_im = mirror[parity, 0, pl.ds(j, 1)], mirror[parity, 1, pl.ds(j, 1)]
+                        out[j, parity, 0, rows] = held[block, parity, 0, 0, j] + sign * (re * m_re + im * m_im)
+                        out[j, parity, 1, rows] = held[block, parity, 0, 1, j] + sign * (re * m_im - im * m_re)
+
+                backward(sides[block, side], parity, twist, tables[parity], grid.at[block, side], put)
+
+    @pl.when(place[0] == 0)
     def _():
         keep = lax.broadcasted_iota(jnp.int32, (SUB, LANES), 0) > 0
+        rows = pl.ds(0, SUB)
         for parity in range(2):
             for j in range(points):
                 w_re, w_im = extra_turn[parity, 0, pl.ds(j, 1)], extra_turn[parity, 1, pl.ds(j, 1)]
-                near = 2.0 * held[parity, 0, 0, j]
-                far = 2.0 * (held[parity, 1, 0, j] * w_re + held[parity, 1, 1, j] * w_im)
-                out[j, parity, 0] = jnp.where(keep, out[j, parity, 0], near)
-                out[j, parity, 1] = jnp.where(keep, out[j, parity, 1], far)
+                near = 2.0 * held[0, parity, 0, 0, j]
+                far = 2.0 * (held[0, parity, 1, 0, j] * w_re + held[0, parity, 1, 1, j] * w_im)
+                out[j, parity, 0, rows] = jnp.where(keep, out[j, parity, 0, rows], near)
+                out[j, parity, 1, rows] = jnp.where(keep, out[j, parity, 1, rows], far)
 
 
 def response_kernel(parts, turns_in, phases_in, back_table, table, turns, phases, out, packed):
@@ -387,7 +393,7 @@
     total = row_count * columns
     short = total // 2
     slots = half // groups
-    tile, narrow = min(2 * LANES, width // 4), LANES
+    tile, wide = min(2 * LANES, width // 4), width // 2
     f32 = jnp.float32
 
     keys, lanes = np.arange(points), np.arange(LANES)
@@ -430,7 +436,7 @@
     chirp_slots = max(SUB, slots // segments)
     holders = slots // chirp_slots
     blocks = chirp_slots // SUB
-    start = jnp.minimum(segment, holders - 1) * blocks
+    start = jnp.minimum(segment, holders - 1)
     place = jnp.stack([position, start]).astype(jnp.int32)
     every = LANES * keys[:, None] + lanes[None, :]
     extra_turn = np.stack(
@@ -439,29 +445,28 @@
     mirror = np.stack(
         [np.stack(turn(every, columns)), np.stack(turn((1 - columns) * (2 * every + 1), 2 * columns))]
     ).astype(np.float32)
+    small = np.stack([twist, mirror, extra_turn])
     cells = (points * SUB, 2 * LANES)
     chirp_columns = call(
         chirp_kernel,
         "chirp_columns",
-        blocks,
-        [
-            pl.BlockSpec((2, SUB, columns), lambda i, place: (0, place[1] + i, 0)),
-            whole(twist.shape),
+        1,
+        [
+            pl.BlockSpec((2, chirp_slots, columns), lambda i, place: (0, place[1], 0)),
+            whole(small.shape),
             whole(swapped_tables.shape),
-            whole(mirror.shape),
-            whole(extra_turn.shape),
         ],
-        pl.BlockSpec((points, 2, 2, SUB, LANES), lambda i, place: (0, 0, 0, i, 0)),
+        whole((points, 2, 2, chirp_slots, LANES)),
         (points, 2, 2, chirp_slots, LANES),
         [
-            pltpu.VMEM((2,) + cells, f32),
-            pltpu.VMEM((2, 2) + cells, f32),
-            pltpu.VMEM((2, 2, 2, points, SUB, LANES), f32),
+            pltpu.VMEM((blocks, 2) + cells, f32),
+            pltpu.VMEM((blocks, 2, 2) + cells, f32),
+            pltpu.VMEM((blocks, 2, 2, 2, points, SUB, LANES), f32),
         ],
         4e8 * blocks,
         3e6,
         scalars=1,
-    )(place, chirp_phase, twist, swapped_tables, mirror, extra_turn)
+    )(place, chirp_phase, small, swapped_tables)
     if holders < segments:
         chirp_columns = jnp.where(segment < holders, chirp_columns, 0.0)
     if count > points:
@@ -568,14 +573,14 @@
     return call(
         gather_kernel,
         "gather",
-        width // narrow,
-        [
-            pl.BlockSpec((count, 2, 2, own_rows, narrow), lambda c: (0, 0, 0, 0, c)),
-            pl.BlockSpec((count, 2, own_rows, narrow), lambda c: (0, 0, 0, c)),
+        width // wide,
+        [
+            pl.BlockSpec((count, 2, 2, own_rows, wide), lambda c: (0, 0, 0, 0, c)),
+            pl.BlockSpec((count, 2, own_rows, wide), lambda c: (0, 0, 0, c)),
             whole(phases.shape),
             whole(back_table.shape),
         ],
-        pl.BlockSpec((1, 2, quarter, narrow), lambda c: (0, 0, 0, c)),
+        pl.BlockSpec((1, 2, quarter, wide), lambda c: (0, 0, 0, c)),
         (1, 2, quarter, width),
         [],
         2e9,

time: 311 us -> 307 us (0.987)
    unnamed x24 -> x20, local copies, waits for them, and re-layouts: 6.48 us -> 4.89 us
where the time goes in v1:
time: 307 us; the launch traced here: 306 us
  waiting for transfers between devices  140 us (46%)
  blocking collectives  97.3 us (32%)
  Pallas kernels  42.7 us (14%)
  starting transfers between devices  16.4 us (5%)
  local copies, waits for them, and re-layouts  9.17 us (3%)
    all_to_all x3, waiting for transfers between devices, exchange(): lax.all_to_all(values, ('seg', 'fft'), split_axis=0, concat_axis=0, tiled...  140 us
    all_to_all x1, blocking collectives, exchange(): lax.all_to_all(values, ('seg', 'fft'), split_axis=0, concat_axis=0, tiled...  97.3 us
    all_to_all x3, starting transfers between devices, exchange(): lax.all_to_all(values, ('seg', 'fft'), split_axis=0, concat_axis=0, tiled...  16.4 us
    pallas_call x1, Pallas kernels, per_device(): call(apply_kernel, 'apply', segments // 2 + 2, [pl.BlockSpec((points, 2,...  10.7 us
    pallas_call x1, Pallas kernels, per_device(): call(response_kernel, 'response', 4, [whole(chirp_parts.shape), whole(chi...  8.57 us
    pallas_call x1, Pallas kernels, per_device(): call(forward_kernel, 'forward', segments // 2, [pl.BlockSpec((2, groups,...  6.64 us
    pallas_call x1, Pallas kernels, per_device(): call(chirp_kernel, 'chirp_columns', 1, [pl.BlockSpec((2, chirp_slots, col...  6.23 us
  transfers between devices with their start and end apart: 3, of which 3 were waited for; matrix products, arithmetic and copies ran while one was open for 1% of the time, Pallas kernels for 7%

profile of v1, /device:TPU:1, one launch (start us, length us, event | category | flops | bytes accessed | tf_op | source)
XLA Modules:
  0.0 305.7 jit_solution(8391977033175509241)
XLA Ops:
  0.0 0.1 pad_add_fusion.place
  0.1 0.0 copy-start.6
  0.1 1.1 copy-done.6
  1.2 0.9 copy-done.7
  2.1 6.2 %chirp_columns.1 = f32[32,2,2,16,128]{4,3,2,1,0:T(8,128)} custom-call(s32[2]{0:T(128)S(1)} %pad_add_fusion.place, f32[2,128,4096]{2,1,0:T(8,128)} %angles.1, f32[3,2,2,32,128]{4,3,2,1,0:T(8,128)S(1)} %copy-done.7, bf16[2,768,256]{2,1,0:T(8,128)(2,1)S(1)} %copy-done.6), custom_call_target="tpu_custom_call" | custom-call | flops 800000000 | bytes 3000000 | tf_op jit(solution)/shard_map/chirp_columns/pallas_call | solution.py:450
  8.4 7.1 %all-to-all-start = ((f32[32,2,2,16,128]{4,3,2,1,0:T(8,128)}), f32[32,2,2,16,128]{4,3,2,1,0:T(8,128)}, u32[]{:S(2)}, u32[]{:S(2)}) async-start(f32[32,2,2,16,128]{4,3,2,1,0:T(8,128)} %chirp_columns.1), calls=%async_computation | async-start | bytes 2097152 | tf_op jit(solution)/shard_map/all_to_all | solution.py:375
  15.5 0.7 dynamic-slice_bitcast_fusion.1
  16.2 0.5 copy.17.phases
  16.8 0.0 copy-done.1
  16.8 0.0 copy-done.5
  16.8 5.5 %spread.1 = f32[32,2,2,8,1024]{4,3,2,1,0:T(8,128)} custom-call(f32[1,2,256,1024]{3,2,1,0:T(8,128)S(1)} %copy-done.1, bf16[512,768]{1,0:T(8,128)(2,1)S(1)} %copy-done.5, f32[32,2,8,1024]{3,2,1,0:T(8,128)} %constant.61.clone.turns, f32[32,4,8,1]{3,2,1,0:T(8,128)S(1)} %copy.17.phases), custom_call_target="tpu_custom_call" | custom-call | flops 2000000000 | bytes 10000000 | tf_op jit(solution)/shard_map/spread/pallas_call | solution.py:516
  22.3 19.6 %all-to-all-done.parts = f32[32,2,2,16,128]{4,3,2,1,0:T(8,128)} async-done(((f32[32,2,2,16,128]{4,3,2,1,0:T(8,128)}), f32[32,2,2,16,128]{4,3,2,1,0:T(8,128)}, u32[]{:S(2)}, u32[]{:S(2)}) %all-to-all-start) | async-done | bytes 1048608 | tf_op jit(solution)/shard_map/all_to_all | solution.py:375
  41.9 3.3 %all-to-all-start.2 = ((f32[32,2,2,8,1024]{4,3,2,1,0:T(8,128)}), f32[32,2,2,8,1024]{4,3,2,1,0:T(8,128)}, u32[]{:S(2)}, u32[]{:S(2)}) async-start(f32[32,2,2,8,1024]{4,3,2,1,0:T(8,128)} %spread.1), calls=%async_computation.2 | async-start | bytes 8388608 | tf_op jit(solution)/shard_map/all_to_all | solution.py:375
  45.3 0.7 dynamic-slice_bitcast_fusion.2
  46.0 0.5 copy.16.phases
  46.5 0.8 dynamic-slice_bitcast_fusion
  47.3 1.0 copy.15.phases_in
  48.3 0.0 copy-done.9
  48.3 8.6 %response.1 = f32[32,4,2,2,8,128]{5,4,3,2,1,0:T(8,128)} custom-call(f32[32,2,2,16,128]{4,3,2,1,0:T(8,128)} %all-to-all-done.parts, f32[32,2,16,128]{3,2,1,0:T(8,128)S(1)} %copy-done.9, f32[32,4,16,1]{3,2,1,0:T(8,128)S(1)} %copy.15.phases_in, bf16[1024,3072]{1,0:T(8,128)(2,1)} %constant.59.clone.back_table, bf16[512,768]{1,0:T(8,128)(2,1)S(1)} %copy-done.5, ...), custom_call_target="tpu_custom_call" | custom-call | flops 5000000000 | bytes 10000000 | tf_op jit(solution)/shard_map/response/pallas_call | solution.py:494
  56.9 80.2 %all-to-all-done.2 = f32[32,2,2,8,1024]{4,3,2,1,0:T(8,128)} async-done(((f32[32,2,2,8,1024]{4,3,2,1,0:T(8,128)}), f32[32,2,2,8,1024]{4,3,2,1,0:T(8,128)}, u32[]{:S(2)}, u32[]{:S(2)}) %all-to-all-start.2) | async-done | bytes 4194336 | tf_op jit(solution)/shard_map/all_to_all | solution.py:375
  137.1 5.9 %all-to-all-start.1 = ((f32[32,4,2,2,8,128]{5,4,3,2,1,0:T(8,128)}), f32[32,4,2,2,8,128]{5,4,3,2,1,0:T(8,128)S(1)}, u32[]{:S(2)}, u32[]{:S(2)}) async-start(f32[32,4,2,2,8,128]{5,4,3,2,1,0:T(8,128)} %response.1), calls=%async_computation.1 | async-start | bytes 4194304 | tf_op jit(solution)/shard_map/all_to_all | solution.py:375
  143.0 0.0 copy-done.8
  143.0 0.0 copy-start.2
  143.0 1.4 copy-done.2
  144.4 6.6 %forward.1.spectrum = f32[8,2,256,256]{3,2,1,0:T(8,128)} custom-call(f32[8,4,2,2,8,1024]{5,4,3,2,1,0:T(8,128)} %bitcast.5.x, f32[2,2,32,128]{3,2,1,0:T(8,128)S(1)} %copy-done.8, bf16[4,768,256]{2,1,0:T(8,128)(2,1)S(1)} %copy-done.2), custom_call_target="tpu_custom_call" | custom-call | flops 2000000000 | bytes 10000000 | tf_op jit(solution)/shard_map/forward/pallas_call | solution.py:535
  151.1 40.2 %all-to-all-done.1.taps = f32[32,4,2,2,8,128]{5,4,3,2,1,0:T(8,128)S(1)} async-done(((f32[32,4,2,2,8,128]{5,4,3,2,1,0:T(8,128)}), f32[32,4,2,2,8,128]{5,4,3,2,1,0:T(8,128)S(1)}, u32[]{:S(2)}, u32[]{:S(2)}) %all-to-all-start.1) | async-done | bytes 2097184 | tf_op jit(solution)/shard_map/all_to_all | solution.py:375
  191.3 1.4 copy-done.3
  192.7 10.7 %apply.1 = f32[8,4,2,2,8,1024]{5,4,3,2,1,0:T(8,128)} custom-call(f32[32,4,2,2,8,128]{5,4,3,2,1,0:T(8,128)S(1)} %all-to-all-done.1.taps, f32[8,2,256,256]{3,2,1,0:T(8,128)} %forward.1.spectrum, f32[2,2,32,128]{3,2,1,0:T(8,128)S(1)} %copy-done.8, bf16[4,768,256]{2,1,0:T(8,128)(2,1)S(1)} %copy-done.3), custom_call_target="tpu_custom_call" | custom-call | flops 4000000000 | bytes 20000000 | tf_op jit(solution)/shard_map/apply/pallas_call | solution.py:550
  203.4 97.3 %all_to_all.20.parts = f32[32,2,2,8,1024]{4,3,2,1,0:T(8,128)} all-to-all(f32[32,2,2,8,1024]{4,3,2,1,0:T(8,128)} %bitcast.10), channel_id=1, replica_groups=mesh['seg'=8,'fft'=4] {'seg','fft'}, dimensions={0} | all-to-all | bytes 8388608 | tf_op jit(solution)/shard_map/all_to_all | solution.py:375
  300.6 0.0 copy-done
  300.6 0.0 copy-done.4
  300.7 5.1 %gather.1 = f32[1,2,256,1024]{3,2,1,0:T(8,128)} custom-call(f32[32,2,2,8,1024]{4,3,2,1,0:T(8,128)} %all_to_all.20.parts, f32[32,2,8,1024]{3,2,1,0:T(8,128)S(1)} %copy-done, f32[32,4,8,1]{3,2,1,0:T(8,128)S(1)} %copy.17.phases, bf16[256,1536]{1,0:T(8,128)(2,1)S(1)} %copy-done.4), custom_call_target="tpu_custom_call" | custom-call | flops 2000000000 | bytes 10000000 | tf_op jit(solution)/shard_map/gather/pallas_call | solution.py:573
  (8 shorter events, 0.0 us)
Async XLA Ops:
  0.1 1.1 copy-start.6
  1.2 0.9 copy-start.7
  2.1 14.6 %copy-start.1 = (f32[1,2,256,1024]{3,2,1,0:T(8,128)S(1)}, f32[1,2,256,1024]{3,2,1,0:T(8,128)}, u32[]{:S(2)}) copy-start(f32[1,2,256,1024]{3,2,1,0:T(8,128)} %x.1) | copy-start | bytes 6291460
  2.1 14.7 %copy-start.5 = (bf16[512,768]{1,0:T(8,128)(2,1)S(1)}, bf16[512,768]{1,0:T(8,128)(2,1)}, u32[]{:S(2)}) copy-start(bf16[512,768]{1,0:T(8,128)(2,1)} %constant.60.clone.table) | copy-start | bytes 2359300
  8.4 33.6 %all-to-all-start = ((f32[32,2,2,16,128]{4,3,2,1,0:T(8,128)}), f32[32,2,2,16,128]{4,3,2,1,0:T(8,128)}, u32[]{:S(2)}, u32[]{:S(2)}) async-start(f32[32,2,2,16,128]{4,3,2,1,0:T(8,128)} %chirp_columns.1), calls=%async_computation | async-start | bytes 2097152 | tf_op jit(solution)/shard_map/all_to_all | solution.py:375
  22.3 26.0 %copy-start.9 = (f32[32,2,16,128]{3,2,1,0:T(8,128)S(1)}, f32[32,2,16,128]{3,2,1,0:T(8,128)}, u32[]{:S(2)}) copy-start(f32[32,2,16,128]{3,2,1,0:T(8,128)} %constant.58.clone.turns_in) | copy-start | bytes 1572868
  41.9 95.2 %all-to-all-start.2 = ((f32[32,2,2,8,1024]{4,3,2,1,0:T(8,128)}), f32[32,2,2,8,1024]{4,3,2,1,0:T(8,128)}, u32[]{:S(2)}, u32[]{:S(2)}) async-start(f32[32,2,2,8,1024]{4,3,2,1,0:T(8,128)} %spread.1), calls=%async_computation.2 | async-start | bytes 8388608 | tf_op jit(solution)/shard_map/all_to_all | solution.py:375
  56.9 86.1 %copy-start.8 = (f32[2,2,32,128]{3,2,1,0:T(8,128)S(1)}, f32[2,2,32,128]{3,2,1,0:T(8,128)}, u32[]{:S(2)}) copy-start(f32[2,2,32,128]{3,2,1,0:T(8,128)} %constant.62.clone.twist) | copy-start | bytes 196612
  137.1 54.2 %all-to-all-start.1 = ((f32[32,4,2,2,8,128]{5,4,3,2,1,0:T(8,128)}), f32[32,4,2,2,8,128]{5,4,3,2,1,0:T(8,128)S(1)}, u32[]{:S(2)}, u32[]{:S(2)}) async-start(f32[32,4,2,2,8,128]{5,4,3,2,1,0:T(8,128)} %response.1), calls=%async_computation.1 | async-start | bytes 4194304 | tf_op jit(solution)/shard_map/all_to_all | solution.py:375
  143.0 1.4 copy-start.2
  191.3 1.4 copy-start.3
  203.3 97.3 %copy-start = (f32[32,2,8,1024]{3,2,1,0:T(8,128)S(1)}, f32[32,2,8,1024]{3,2,1,0:T(8,128)}, u32[]{:S(2)}) copy-start(f32[32,2,8,1024]{3,2,1,0:T(8,128)} %constant.61.clone.turns) | copy-start | bytes 6291460
  203.3 97.3 %copy-start.4 = (bf16[256,1536]{1,0:T(8,128)(2,1)S(1)}, bf16[256,1536]{1,0:T(8,128)(2,1)}, u32[]{:S(2)}) copy-start(bf16[256,1536]{1,0:T(8,128)(2,1)} %constant.64.clone.table) | copy-start | bytes 2359300

commit v2 on v1

--- a/solution.py
+++ b/solution.py
@@ -100,29 +100,34 @@
     return result
 
 
-def forward(value_at, twist, tables, grid):
+def forward(value_ats, twist, tables, grid):
+    points = twist.shape[2]
     spectra = []
     for parity in range(2):
-        values = [value_at(parity, j) for j in range(twist.shape[2])]
-        for k, (re, im) in enumerate(small_dft(values, -1)):
-            w_re, w_im = twist[parity, 0, pl.ds(k, 1)], twist[parity, 1, pl.ds(k, 1)]
-            grid[parity, pl.ds(k * SUB, SUB), pl.ds(0, LANES)] = re * w_re - im * w_im
-            grid[parity, pl.ds(k * SUB, SUB), pl.ds(LANES, LANES)] = re * w_im + im * w_re
+        for n, value_at in enumerate(value_ats):
+            values = [value_at(parity, j) for j in range(points)]
+            for k, (re, im) in enumerate(small_dft(values, -1)):
+                w_re, w_im = twist[parity, 0, pl.ds(k, 1)], twist[parity, 1, pl.ds(k, 1)]
+                rows = pl.ds((n * points + k) * SUB, SUB)
+                grid[parity, rows, pl.ds(0, LANES)] = re * w_re - im * w_im
+                grid[parity, rows, pl.ds(LANES, LANES)] = re * w_im + im * w_re
         spectra.append(dot(thrice(grid[parity], 1), tables[parity]))
     even, odd = spectra
     return even + odd, even - odd
 
 
-def backward(side, parity, twist, table, grid, put):
+def backward(side, parity, twist, table, grid, puts):
+    points = twist.shape[2]
     grid[parity] = dot(thrice(side, 1), table)
-    values = []
-    for k in range(twist.shape[2]):
-        re = grid[parity, pl.ds(k * SUB, SUB), pl.ds(0, LANES)]
-        im = grid[parity, pl.ds(k * SUB, SUB), pl.ds(LANES, LANES)]
-        w_re, w_im = twist[parity, 0, pl.ds(k, 1)], twist[parity, 1, pl.ds(k, 1)]
-        values.append((re * w_re + im * w_im, im * w_re - re * w_im))
-    for j, (re, im) in enumerate(small_dft(values, 1)):
-        put(j, re, im)
+    for n, put in enumerate(puts):
+        values = []
+        for k in range(points):
+            rows = pl.ds((n * points + k) * SUB, SUB)
+            re, im = grid[parity, rows, pl.ds(0, LANES)], grid[parity, rows, pl.ds(LANES, LANES)]
+            w_re, w_im = twist[parity, 0, pl.ds(k, 1)], twist[parity, 1, pl.ds(k, 1)]
+            values.append((re * w_re + im * w_im, im * w_re - re * w_im))
+        for j, (re, im) in enumerate(small_dft(values, 1)):
+            put(j, re, im)
 
 
 def turned_by(angles):
@@ -177,8 +182,9 @@
             tiles = [angles[side, rows, pl.ds(k * LANES, LANES)] for k in range(points)]
             for k, value in enumerate(digits_swapped(tiles)):
                 cos, sin = turned_by(value)
-                sides[block, side, pl.ds(k * SUB, SUB), pl.ds(0, LANES)] = cos
-                sides[block, side, pl.ds(k * SUB, SUB), pl.ds(LANES, LANES)] = sin
+                cell = pl.ds(((2 * block + side) * points + k) * SUB, SUB)
+                sides[cell, pl.ds(0, LANES)] = cos
+                sides[cell, pl.ds(LANES, LANES)] = sin
 
     @pl.when(place[0] == 0)
     def _():
@@ -187,11 +193,12 @@
         alive = jnp.logical_or(slot > 0, lane > 0)
         for part in range(2):
             lanes = pl.ds(part * LANES, LANES)
-            sides[0, 0, pl.ds(0, SUB), lanes] = jnp.where(alive, sides[0, 0, pl.ds(0, SUB), lanes], 0.0)
-
-    for block in range(blocks):
-        rows = pl.ds(block * SUB, SUB)
-        for parity in range(2):
+            sides[pl.ds(0, SUB), lanes] = jnp.where(alive, sides[pl.ds(0, SUB), lanes], 0.0)
+
+    for parity in range(2):
+        puts = []
+        for block in range(blocks):
+            rows = pl.ds(block * SUB, SUB)
             for side in range(2):
 
                 def put(j, re, im, block=block, rows=rows, parity=parity, side=side):
@@ -203,7 +210,8 @@
                         out[j, parity, 0, rows] = held[block, parity, 0, 0, j] + sign * (re * m_re + im * m_im)
                         out[j, parity, 1, rows] = held[block, parity, 0, 1, j] + sign * (re * m_im - im * m_re)
 
-                backward(sides[block, side], parity, twist, tables[parity], grid.at[block, side], put)
+                puts.append(put)
+        backward(sides[...], parity, twist, tables[parity], grid, puts)
 
     @pl.when(place[0] == 0)
     def _():
@@ -253,6 +261,8 @@
 
 def forward_kernel(x, twist, tables, out, grid):
     tiles = x.shape[5] // LANES
+    size = out.shape[2]
+    value_ats = []
     for n in range(x.shape[0]):
 
         def value_at(parity, j, n=n):
@@ -260,15 +270,18 @@
             lanes = pl.ds(tile * LANES, LANES)
             return x[n, group, parity, 0, :, lanes], x[n, group, parity, 1, :, lanes]
 
-        upper, lower = forward(value_at, twist, tables, grid.at[n])
-        out[n, 0] = upper
-        out[n, 1] = lower
+        value_ats.append(value_at)
+    upper, lower = forward(value_ats, twist, tables, grid)
+    for n in range(x.shape[0]):
+        out[n, 0] = upper[n * size : (n + 1) * size]
+        out[n, 1] = lower[n * size : (n + 1) * size]
 
 
 def apply_kernel(taps, spectrum, twist, tables, out, raw, response, past, sides, grid):
     step = pl.program_id(0)
     points = twist.shape[2]
     tiles = out.shape[5] // LANES
+    size = points * SUB
     re_lanes, im_lanes = pl.ds(0, LANES), pl.ds(LANES, LANES)
 
     @pl.when(step == 0)
@@ -277,14 +290,17 @@
 
     @pl.when(step < 2)
     def _():
+        value_ats = []
         for n in range(2):
 
             def value_at(parity, j, n=n):
                 return taps[j, n, parity, 0], taps[j, n, parity, 1]
 
-            upper, lower = forward(value_at, twist, tables, grid.at[n])
-            raw[2 * step + n, 0] = upper
-            raw[2 * step + n, 1] = lower
+            value_ats.append(value_at)
+        upper, lower = forward(value_ats, twist, tables, grid)
+        for n in range(2):
+            raw[2 * step + n, 0] = upper[n * size : (n + 1) * size]
+            raw[2 * step + n, 1] = lower[n * size : (n + 1) * size]
 
     @pl.when(step == 1)
     def _():
@@ -317,10 +333,12 @@
                     sums[n].append(totals[n])
             for n in range(2):
                 for parity, value in enumerate((plus(*sums[n]), minus(*sums[n]))):
-                    sides[n, parity, rows, re_lanes] = value[0]
-                    sides[n, parity, rows, im_lanes] = value[1]
-        for n in range(2):
-            for parity in range(2):
+                    cell = pl.ds(n * size + k * SUB, SUB)
+                    sides[parity, cell, re_lanes] = value[0]
+                    sides[parity, cell, im_lanes] = value[1]
+        for parity in range(2):
+            puts = []
+            for n in range(2):
 
                 def put(j, re, im, n=n, parity=parity):
                     group, tile = divmod(j, tiles)
@@ -328,7 +346,8 @@
                     out[n, group, parity, 0, :, lanes] = re
                     out[n, group, parity, 1, :, lanes] = im
 
-                backward(sides[n, parity], parity, twist, tables[2 + parity], grid.at[n], put)
+                puts.append(put)
+            backward(sides[parity], parity, twist, tables[2 + parity], grid, puts)
         past[0] = past[2]
         past[1] = spectrum[0]
         past[2] = spectrum[1]
@@ -459,8 +478,8 @@
         whole((points, 2, 2, chirp_slots, LANES)),
         (points, 2, 2, chirp_slots, LANES),
         [
-            pltpu.VMEM((blocks, 2) + cells, f32),
-            pltpu.VMEM((blocks, 2, 2) + cells, f32),
+            pltpu.VMEM((2 * blocks * points * SUB, 2 * LANES), f32),
+            pltpu.VMEM((2, 2 * blocks * points * SUB, 2 * LANES), f32),
             pltpu.VMEM((blocks, 2, 2, 2, points, SUB, LANES), f32),
         ],
         4e8 * blocks,
@@ -531,7 +550,7 @@
     )(voltage, row_table, turns, phases)
     spread = exchange(spread).reshape(segments, groups, 2, 2, own_rows, width)
 
-    pair_scratch = pltpu.VMEM((2, 2) + cells, f32)
+    pair_scratch = pltpu.VMEM((2, 2 * points * SUB, 2 * LANES), f32)
     spectrum = call(
         forward_kernel,
         "forward",

time: 307 us -> 307 us (level)
  no operation moved by 1% of the time
where the time goes in v2:
time: 307 us; the launch traced here: 306 us
  waiting for transfers between devices  140 us (46%)
  blocking collectives  97.3 us (32%)
  Pallas kernels  42.7 us (14%)
  starting transfers between devices  16.4 us (5%)
  local copies, waits for them, and re-layouts  9.17 us (3%)
    all_to_all x3, waiting for transfers between devices, exchange(): lax.all_to_all(values, ('seg', 'fft'), split_axis=0, concat_axis=0, tiled...  140 us
    all_to_all x1, blocking collectives, exchange(): lax.all_to_all(values, ('seg', 'fft'), split_axis=0, concat_axis=0, tiled...  97.3 us
    all_to_all x3, starting transfers between devices, exchange(): lax.all_to_all(values, ('seg', 'fft'), split_axis=0, concat_axis=0, tiled...  16.4 us
    pallas_call x1, Pallas kernels, per_device(): call(apply_kernel, 'apply', segments // 2 + 2, [pl.BlockSpec((points, 2,...  10.7 us
    pallas_call x1, Pallas kernels, per_device(): call(response_kernel, 'response', 4, [whole(chirp_parts.shape), whole(chi...  8.58 us
    pallas_call x1, Pallas kernels, per_device(): call(forward_kernel, 'forward', segments // 2, [pl.BlockSpec((2, groups,...  6.64 us
    pallas_call x1, Pallas kernels, per_device(): call(chirp_kernel, 'chirp_columns', 1, [pl.BlockSpec((2, chirp_slots, col...  6.26 us
  transfers between devices with their start and end apart: 3, of which 3 were waited for; matrix products, arithmetic and copies ran while one was open for 1% of the time, Pallas kernels for 7%

profile of v2, /device:TPU:1, one launch (start us, length us, event | category | flops | bytes accessed | tf_op | source)
XLA Modules:
  0.0 305.7 jit_solution(7217845009585898851)
XLA Ops:
  0.0 0.1 pad_add_fusion.place
  0.1 0.0 copy-start.6
  0.1 1.1 copy-done.6
  1.2 0.9 copy-done.7
  2.1 6.3 %chirp_columns.1 = f32[32,2,2,16,128]{4,3,2,1,0:T(8,128)} custom-call(s32[2]{0:T(128)S(1)} %pad_add_fusion.place, f32[2,128,4096]{2,1,0:T(8,128)} %angles.1, f32[3,2,2,32,128]{4,3,2,1,0:T(8,128)S(1)} %copy-done.7, bf16[2,768,256]{2,1,0:T(8,128)(2,1)S(1)} %copy-done.6), custom_call_target="tpu_custom_call" | custom-call | flops 800000000 | bytes 3000000 | tf_op jit(solution)/shard_map/chirp_columns/pallas_call | solution.py:469
  8.4 7.1 %all-to-all-start = ((f32[32,2,2,16,128]{4,3,2,1,0:T(8,128)}), f32[32,2,2,16,128]{4,3,2,1,0:T(8,128)}, u32[]{:S(2)}, u32[]{:S(2)}) async-start(f32[32,2,2,16,128]{4,3,2,1,0:T(8,128)} %chirp_columns.1), calls=%async_computation | async-start | bytes 2097152 | tf_op jit(solution)/shard_map/all_to_all | solution.py:394
  15.6 0.7 dynamic-slice_bitcast_fusion.1
  16.3 0.5 copy.17.phases
  16.8 0.0 copy-done.1
  16.8 0.0 copy-done.5
  16.8 5.5 %spread.1 = f32[32,2,2,8,1024]{4,3,2,1,0:T(8,128)} custom-call(f32[1,2,256,1024]{3,2,1,0:T(8,128)S(1)} %copy-done.1, bf16[512,768]{1,0:T(8,128)(2,1)S(1)} %copy-done.5, f32[32,2,8,1024]{3,2,1,0:T(8,128)} %constant.61.clone.turns, f32[32,4,8,1]{3,2,1,0:T(8,128)S(1)} %copy.17.phases), custom_call_target="tpu_custom_call" | custom-call | flops 2000000000 | bytes 10000000 | tf_op jit(solution)/shard_map/spread/pallas_call | solution.py:535
  22.3 19.6 %all-to-all-done.parts = f32[32,2,2,16,128]{4,3,2,1,0:T(8,128)} async-done(((f32[32,2,2,16,128]{4,3,2,1,0:T(8,128)}), f32[32,2,2,16,128]{4,3,2,1,0:T(8,128)}, u32[]{:S(2)}, u32[]{:S(2)}) %all-to-all-start) | async-done | bytes 1048608 | tf_op jit(solution)/shard_map/all_to_all | solution.py:394
  42.0 3.3 %all-to-all-start.2 = ((f32[32,2,2,8,1024]{4,3,2,1,0:T(8,128)}), f32[32,2,2,8,1024]{4,3,2,1,0:T(8,128)}, u32[]{:S(2)}, u32[]{:S(2)}) async-start(f32[32,2,2,8,1024]{4,3,2,1,0:T(8,128)} %spread.1), calls=%async_computation.2 | async-start | bytes 8388608 | tf_op jit(solution)/shard_map/all_to_all | solution.py:394
  45.3 0.7 dynamic-slice_bitcast_fusion.2
  46.0 0.5 copy.16.phases
  46.6 0.8 dynamic-slice_bitcast_fusion
  47.3 1.0 copy.15.phases_in
  48.3 0.0 copy-done.9
  48.3 8.6 %response.1 = f32[32,4,2,2,8,128]{5,4,3,2,1,0:T(8,128)} custom-call(f32[32,2,2,16,128]{4,3,2,1,0:T(8,128)} %all-to-all-done.parts, f32[32,2,16,128]{3,2,1,0:T(8,128)S(1)} %copy-done.9, f32[32,4,16,1]{3,2,1,0:T(8,128)S(1)} %copy.15.phases_in, bf16[1024,3072]{1,0:T(8,128)(2,1)} %constant.59.clone.back_table, bf16[512,768]{1,0:T(8,128)(2,1)S(1)} %copy-done.5, ...), custom_call_target="tpu_custom_call" | custom-call | flops 5000000000 | bytes 10000000 | tf_op jit(solution)/shard_map/response/pallas_call | solution.py:513
  56.9 80.2 %all-to-all-done.2 = f32[32,2,2,8,1024]{4,3,2,1,0:T(8,128)} async-done(((f32[32,2,2,8,1024]{4,3,2,1,0:T(8,128)}), f32[32,2,2,8,1024]{4,3,2,1,0:T(8,128)}, u32[]{:S(2)}, u32[]{:S(2)}) %all-to-all-start.2) | async-done | bytes 4194336 | tf_op jit(solution)/shard_map/all_to_all | solution.py:394
  137.1 5.9 %all-to-all-start.1 = ((f32[32,4,2,2,8,128]{5,4,3,2,1,0:T(8,128)}), f32[32,4,2,2,8,128]{5,4,3,2,1,0:T(8,128)S(1)}, u32[]{:S(2)}, u32[]{:S(2)}) async-start(f32[32,4,2,2,8,128]{5,4,3,2,1,0:T(8,128)} %response.1), calls=%async_computation.1 | async-start | bytes 4194304 | tf_op jit(solution)/shard_map/all_to_all | solution.py:394
  143.1 0.0 copy-done.8
  143.1 0.0 copy-start.2
  143.1 1.4 copy-done.2
  144.5 6.6 %forward.1.spectrum = f32[8,2,256,256]{3,2,1,0:T(8,128)} custom-call(f32[8,4,2,2,8,1024]{5,4,3,2,1,0:T(8,128)} %bitcast.5.x, f32[2,2,32,128]{3,2,1,0:T(8,128)S(1)} %copy-done.8, bf16[4,768,256]{2,1,0:T(8,128)(2,1)S(1)} %copy-done.2), custom_call_target="tpu_custom_call" | custom-call | flops 2000000000 | bytes 10000000 | tf_op jit(solution)/shard_map/forward/pallas_call | solution.py:554
  151.1 40.2 %all-to-all-done.1.taps = f32[32,4,2,2,8,128]{5,4,3,2,1,0:T(8,128)S(1)} async-done(((f32[32,4,2,2,8,128]{5,4,3,2,1,0:T(8,128)}), f32[32,4,2,2,8,128]{5,4,3,2,1,0:T(8,128)S(1)}, u32[]{:S(2)}, u32[]{:S(2)}) %all-to-all-start.1) | async-done | bytes 2097184 | tf_op jit(solution)/shard_map/all_to_all | solution.py:394
  191.3 1.4 copy-done.3
  192.7 10.7 %apply.1 = f32[8,4,2,2,8,1024]{5,4,3,2,1,0:T(8,128)} custom-call(f32[32,4,2,2,8,128]{5,4,3,2,1,0:T(8,128)S(1)} %all-to-all-done.1.taps, f32[8,2,256,256]{3,2,1,0:T(8,128)} %forward.1.spectrum, f32[2,2,32,128]{3,2,1,0:T(8,128)S(1)} %copy-done.8, bf16[4,768,256]{2,1,0:T(8,128)(2,1)S(1)} %copy-done.3), custom_call_target="tpu_custom_call" | custom-call | flops 4000000000 | bytes 20000000 | tf_op jit(solution)/shard_map/apply/pallas_call | solution.py:569
  203.4 97.3 %all_to_all.20.parts = f32[32,2,2,8,1024]{4,3,2,1,0:T(8,128)} all-to-all(f32[32,2,2,8,1024]{4,3,2,1,0:T(8,128)} %bitcast.10), channel_id=1, replica_groups=mesh['seg'=8,'fft'=4] {'seg','fft'}, dimensions={0} | all-to-all | bytes 8388608 | tf_op jit(solution)/shard_map/all_to_all | solution.py:394
  300.7 0.0 copy-done
  300.7 0.0 copy-done.4
  300.7 5.1 %gather.1 = f32[1,2,256,1024]{3,2,1,0:T(8,128)} custom-call(f32[32,2,2,8,1024]{4,3,2,1,0:T(8,128)} %all_to_all.20.parts, f32[32,2,8,1024]{3,2,1,0:T(8,128)S(1)} %copy-done, f32[32,4,8,1]{3,2,1,0:T(8,128)S(1)} %copy.17.phases, bf16[256,1536]{1,0:T(8,128)(2,1)S(1)} %copy-done.4), custom_call_target="tpu_custom_call" | custom-call | flops 2000000000 | bytes 10000000 | tf_op jit(solution)/shard_map/gather/pallas_call | solution.py:592
  (8 shorter events, 0.0 us)
Async XLA Ops:
  0.1 1.1 copy-start.6
  1.2 0.9 copy-start.7
  2.1 14.7 %copy-start.1 = (f32[1,2,256,1024]{3,2,1,0:T(8,128)S(1)}, f32[1,2,256,1024]{3,2,1,0:T(8,128)}, u32[]{:S(2)}) copy-start(f32[1,2,256,1024]{3,2,1,0:T(8,128)} %x.1) | copy-start | bytes 6291460
  2.1 14.7 %copy-start.5 = (bf16[512,768]{1,0:T(8,128)(2,1)S(1)}, bf16[512,768]{1,0:T(8,128)(2,1)}, u32[]{:S(2)}) copy-start(bf16[512,768]{1,0:T(8,128)(2,1)} %constant.60.clone.table) | copy-start | bytes 2359300
  8.4 33.6 %all-to-all-start = ((f32[32,2,2,16,128]{4,3,2,1,0:T(8,128)}), f32[32,2,2,16,128]{4,3,2,1,0:T(8,128)}, u32[]{:S(2)}, u32[]{:S(2)}) async-start(f32[32,2,2,16,128]{4,3,2,1,0:T(8,128)} %chirp_columns.1), calls=%async_computation | async-start | bytes 2097152 | tf_op jit(solution)/shard_map/all_to_all | solution.py:394
  22.3 26.0 %copy-start.9 = (f32[32,2,16,128]{3,2,1,0:T(8,128)S(1)}, f32[32,2,16,128]{3,2,1,0:T(8,128)}, u32[]{:S(2)}) copy-start(f32[32,2,16,128]{3,2,1,0:T(8,128)} %constant.58.clone.turns_in) | copy-start | bytes 1572868
  42.0 95.2 %all-to-all-start.2 = ((f32[32,2,2,8,1024]{4,3,2,1,0:T(8,128)}), f32[32,2,2,8,1024]{4,3,2,1,0:T(8,128)}, u32[]{:S(2)}, u32[]{:S(2)}) async-start(f32[32,2,2,8,1024]{4,3,2,1,0:T(8,128)} %spread.1), calls=%async_computation.2 | async-start | bytes 8388608 | tf_op jit(solution)/shard_map/all_to_all | solution.py:394
  56.9 86.1 %copy-start.8 = (f32[2,2,32,128]{3,2,1,0:T(8,128)S(1)}, f32[2,2,32,128]{3,2,1,0:T(8,128)}, u32[]{:S(2)}) copy-start(f32[2,2,32,128]{3,2,1,0:T(8,128)} %constant.62.clone.twist) | copy-start | bytes 196612
  137.1 54.2 %all-to-all-start.1 = ((f32[32,4,2,2,8,128]{5,4,3,2,1,0:T(8,128)}), f32[32,4,2,2,8,128]{5,4,3,2,1,0:T(8,128)S(1)}, u32[]{:S(2)}, u32[]{:S(2)}) async-start(f32[32,4,2,2,8,128]{5,4,3,2,1,0:T(8,128)} %response.1), calls=%async_computation.1 | async-start | bytes 4194304 | tf_op jit(solution)/shard_map/all_to_all | solution.py:394
  143.1 1.4 copy-start.2
  191.3 1.4 copy-start.3
  203.4 97.3 %copy-start = (f32[32,2,8,1024]{3,2,1,0:T(8,128)S(1)}, f32[32,2,8,1024]{3,2,1,0:T(8,128)}, u32[]{:S(2)}) copy-start(f32[32,2,8,1024]{3,2,1,0:T(8,128)} %constant.61.clone.turns) | copy-start | bytes 6291460
  203.4 97.3 %copy-start.4 = (bf16[256,1536]{1,0:T(8,128)(2,1)S(1)}, bf16[256,1536]{1,0:T(8,128)(2,1)}, u32[]{:S(2)}) copy-start(bf16[256,1536]{1,0:T(8,128)(2,1)} %constant.64.clone.table) | copy-start | bytes 2359300

commit v3 on v2

--- a/solution.py
+++ b/solution.py
@@ -11,7 +11,7 @@
 
 LANES = 128
 SUB = 8
-VMEM = 50 * 1024 * 1024
+VMEM = 40 * 1024 * 1024
 
 
 def turn(products, period):

time: 307 us -> 307 us (level)
  local copies, waits for them, and re-layouts: 9.17 us -> 28 us
  Pallas kernels: 42.7 us -> 33.7 us
  waiting for transfers between devices: 140 us -> 131 us
    unnamed x20 -> x36, local copies, waits for them, and re-layouts: 4.89 us -> 22.2 us
    all_to_all x3, waiting for transfers between devices: 140 us -> 131 us  [exchange(): lax.all_to_all(values, ('seg', 'fft'), split_axis=0, concat_axis=0, tiled...]
  transfers between devices with their start and end apart: 3 -> 3, of which waited for: 3 -> 3; matrix products, arithmetic and copies ran while one was open for 1% -> 2% of each run, Pallas kernels for 7% -> 5%
where the time goes in v3:
time: 307 us; the launch traced here: 306 us
  waiting for transfers between devices  131 us (43%)
  blocking collectives  97 us (32%)
  Pallas kernels  33.7 us (11%)
  local copies, waits for them, and re-layouts  28 us (9%)
  starting transfers between devices  16.4 us (5%)
    all_to_all x3, waiting for transfers between devices, exchange(): lax.all_to_all(values, ('seg', 'fft'), split_axis=0, concat_axis=0, tiled...  131 us
    all_to_all x1, blocking collectives, exchange(): lax.all_to_all(values, ('seg', 'fft'), split_axis=0, concat_axis=0, tiled...  97 us
    unnamed x36, local copies, waits for them, and re-layouts  22.2 us
    all_to_all x3, starting transfers between devices, exchange(): lax.all_to_all(values, ('seg', 'fft'), split_axis=0, concat_axis=0, tiled...  16.4 us
    pallas_call x1, Pallas kernels, per_device(): call(apply_kernel, 'apply', segments // 2 + 2, [pl.BlockSpec((points, 2,...  9.51 us
    pallas_call x1, Pallas kernels, per_device(): call(response_kernel, 'response', 4, [whole(chirp_parts.shape), whole(chi...  6.98 us
  transfers between devices with their start and end apart: 3, of which 3 were waited for; matrix products, arithmetic and copies ran while one was open for 2% of the time, Pallas kernels for 5%

profile of v3, /device:TPU:1, one launch (start us, length us, event | category | flops | bytes accessed | tf_op | source)
XLA Modules:
  0.0 306.3 jit_solution(4060366226958725430)
XLA Ops:
  0.1 2.2 copy-done.2
  2.3 1.1 copy-done.12
  3.4 0.9 copy-done.14
  4.3 4.9 %chirp_columns.1 = f32[32,2,2,16,128]{4,3,2,1,0:T(8,128)} custom-call(s32[2]{0:T(128)S(1)} %pad_add_fusion.place, f32[2,128,4096]{2,1,0:T(8,128)S(1)} %copy-done.2, f32[3,2,2,32,128]{4,3,2,1,0:T(8,128)S(1)} %copy-done.14, bf16[2,768,256]{2,1,0:T(8,128)(2,1)S(1)} %copy-done.12), custom_call_target="tpu_custom_call" | custom-call | flops 800000000 | bytes 3000000 | tf_op jit(solution)/shard_map/chirp_columns/pallas_call | solution.py:469
  9.2 7.1 %all-to-all-start = ((f32[32,2,2,16,128]{4,3,2,1,0:T(8,128)}), f32[32,2,2,16,128]{4,3,2,1,0:T(8,128)}, u32[]{:S(2)}, u32[]{:S(2)}) async-start(f32[32,2,2,16,128]{4,3,2,1,0:T(8,128)} %chirp_columns.1), calls=%async_computation | async-start | bytes 2097152 | tf_op jit(solution)/shard_map/all_to_all | solution.py:394
  16.4 0.7 dynamic-slice_bitcast_fusion.1
  17.7 1.6 copy-done.5
  19.3 3.1 %spread.1 = f32[32,2,2,8,1024]{4,3,2,1,0:T(8,128)S(1)} custom-call(f32[1,2,256,1024]{3,2,1,0:T(8,128)S(1)} %copy-done.5, bf16[512,768]{1,0:T(8,128)(2,1)S(1)} %copy-done.11, f32[32,2,8,1024]{3,2,1,0:T(8,128)S(1)} %copy-done.1, f32[32,4,8,1]{3,2,1,0:T(8,128)S(1)} %copy.17.phases), custom_call_target="tpu_custom_call" | custom-call | flops 2000000000 | bytes 10000000 | tf_op jit(solution)/shard_map/spread/pallas_call | solution.py:535
  22.4 2.0 copy-done
  24.4 18.4 %all-to-all-done.parts = f32[32,2,2,16,128]{4,3,2,1,0:T(8,128)} async-done(((f32[32,2,2,16,128]{4,3,2,1,0:T(8,128)}), f32[32,2,2,16,128]{4,3,2,1,0:T(8,128)}, u32[]{:S(2)}, u32[]{:S(2)}) %all-to-all-start) | async-done | bytes 1048608 | tf_op jit(solution)/shard_map/all_to_all | solution.py:394
  42.8 3.3 %all-to-all-start.2 = ((f32[32,2,2,8,1024]{4,3,2,1,0:T(8,128)}), f32[32,2,2,8,1024]{4,3,2,1,0:T(8,128)}, u32[]{:S(2)}, u32[]{:S(2)}) async-start(f32[32,2,2,8,1024]{4,3,2,1,0:T(8,128)} %copy-done), calls=%async_computation.2 | async-start | bytes 8388608 | tf_op jit(solution)/shard_map/all_to_all | solution.py:394
  46.2 0.7 dynamic-slice_bitcast_fusion.2
  46.9 1.3 copy.16.phases
  48.1 0.8 dynamic-slice_bitcast_fusion
  48.9 1.8 copy.15.phases_in
  50.7 1.2 copy-done.9
  52.0 1.0 copy-done.13
  53.0 2.8 copy-done.16
  55.8 1.0 copy-done.17
  56.8 7.0 %response.1 = f32[32,4,2,2,8,128]{5,4,3,2,1,0:T(8,128)S(1)} custom-call(f32[32,2,2,16,128]{4,3,2,1,0:T(8,128)} %all-to-all-done.parts, f32[32,2,16,128]{3,2,1,0:T(8,128)S(1)} %copy-done.17, f32[32,4,16,1]{3,2,1,0:T(8,128)S(1)} %copy-done.9, bf16[1024,3072]{1,0:T(8,128)(2,1)S(1)} %copy-done.16, bf16[512,768]{1,0:T(8,128)(2,1)S(1)} %copy-done.11, ...), custom_call_target="tpu_custom_call" | custom-call | flops 5000000000 | bytes 10000000 | tf_op jit(solution)/shard_map/response/pallas_call | solution.py:513
  63.8 1.3 copy-done.6
  65.1 72.9 %all-to-all-done.2 = f32[32,2,2,8,1024]{4,3,2,1,0:T(8,128)} async-done(((f32[32,2,2,8,1024]{4,3,2,1,0:T(8,128)}), f32[32,2,2,8,1024]{4,3,2,1,0:T(8,128)}, u32[]{:S(2)}, u32[]{:S(2)}) %all-to-all-start.2) | async-done | bytes 4194336 | tf_op jit(solution)/shard_map/all_to_all | solution.py:394
  138.0 6.0 %all-to-all-start.1 = ((f32[32,4,2,2,8,128]{5,4,3,2,1,0:T(8,128)}), f32[32,4,2,2,8,128]{5,4,3,2,1,0:T(8,128)}, u32[]{:S(2)}, u32[]{:S(2)}) async-start(f32[32,4,2,2,8,128]{5,4,3,2,1,0:T(8,128)} %copy-done.6), calls=%async_computation.1 | async-start | bytes 4194304 | tf_op jit(solution)/shard_map/all_to_all | solution.py:394
  144.0 1.4 copy-done.7
  145.4 5.2 %forward.1.spectrum = f32[8,2,256,256]{3,2,1,0:T(8,128)S(1)} custom-call(f32[8,4,2,2,8,1024]{5,4,3,2,1,0:T(8,128)} %bitcast.5.x, f32[2,2,32,128]{3,2,1,0:T(8,128)S(1)} %copy-done.15, bf16[4,768,256]{2,1,0:T(8,128)(2,1)S(1)} %copy-done.7), custom_call_target="tpu_custom_call" | custom-call | flops 2000000000 | bytes 10000000 | tf_op jit(solution)/shard_map/forward/pallas_call | solution.py:554
  150.6 1.9 copy-done.3
  152.6 39.7 %all-to-all-done.1.taps = f32[32,4,2,2,8,128]{5,4,3,2,1,0:T(8,128)} async-done(((f32[32,4,2,2,8,128]{5,4,3,2,1,0:T(8,128)}), f32[32,4,2,2,8,128]{5,4,3,2,1,0:T(8,128)}, u32[]{:S(2)}, u32[]{:S(2)}) %all-to-all-start.1) | async-done | bytes 2097184 | tf_op jit(solution)/shard_map/all_to_all | solution.py:394
  192.3 2.2 copy-done.4
  194.4 1.4 copy-done.8
  195.9 9.5 %apply.1 = f32[8,4,2,2,8,1024]{5,4,3,2,1,0:T(8,128)S(1)} custom-call(f32[32,4,2,2,8,128]{5,4,3,2,1,0:T(8,128)} %all-to-all-done.1.taps, f32[8,2,256,256]{3,2,1,0:T(8,128)S(1)} %copy-done.4, f32[2,2,32,128]{3,2,1,0:T(8,128)S(1)} %copy-done.15, bf16[4,768,256]{2,1,0:T(8,128)(2,1)S(1)} %copy-done.8), custom_call_target="tpu_custom_call" | custom-call | flops 4000000000 | bytes 20000000 | tf_op jit(solution)/shard_map/apply/pallas_call | solution.py:569
  205.4 97.0 %all_to_all.20.parts = f32[32,2,2,8,1024]{4,3,2,1,0:T(8,128)S(1)} all-to-all(f32[32,2,2,8,1024]{4,3,2,1,0:T(8,128)S(1)} %bitcast.10), channel_id=1, replica_groups=mesh['seg'=8,'fft'=4] {'seg','fft'}, dimensions={0} | all-to-all | bytes 8388608 | tf_op jit(solution)/shard_map/all_to_all | solution.py:394
  302.4 3.9 %gather.1 = f32[1,2,256,1024]{3,2,1,0:T(8,128)} custom-call(f32[32,2,2,8,1024]{4,3,2,1,0:T(8,128)S(1)} %all_to_all.20.parts, f32[32,2,8,1024]{3,2,1,0:T(8,128)S(1)} %copy-done.1, f32[32,4,8,1]{3,2,1,0:T(8,128)S(1)} %copy.17.phases, bf16[256,1536]{1,0:T(8,128)(2,1)S(1)} %copy-done.10), custom_call_target="tpu_custom_call" | custom-call | flops 2000000000 | bytes 10000000 | tf_op jit(solution)/shard_map/gather/pallas_call | solution.py:592
  (24 shorter events, 0.7 us)
Async XLA Ops:
  0.1 2.2 copy-start.2
  2.3 1.1 copy-start.12
  3.4 0.9 copy-start.14
  4.3 13.3 %copy-start.1 = (f32[32,2,8,1024]{3,2,1,0:T(8,128)S(1)}, f32[32,2,8,1024]{3,2,1,0:T(8,128)}, u32[]{:S(2)}) copy-start(f32[32,2,8,1024]{3,2,1,0:T(8,128)} %constant.61.clone.turns) | copy-start | bytes 6291460
  4.3 13.3 %copy-start.11 = (bf16[512,768]{1,0:T(8,128)(2,1)S(1)}, bf16[512,768]{1,0:T(8,128)(2,1)}, u32[]{:S(2)}) copy-start(bf16[512,768]{1,0:T(8,128)(2,1)} %constant.60.clone.table) | copy-start | bytes 2359300
  9.2 33.6 %all-to-all-start = ((f32[32,2,2,16,128]{4,3,2,1,0:T(8,128)}), f32[32,2,2,16,128]{4,3,2,1,0:T(8,128)}, u32[]{:S(2)}, u32[]{:S(2)}) async-start(f32[32,2,2,16,128]{4,3,2,1,0:T(8,128)} %chirp_columns.1), calls=%async_computation | async-start | bytes 2097152 | tf_op jit(solution)/shard_map/all_to_all | solution.py:394
  17.7 1.6 copy-start.5
  22.4 2.0 copy-start
  42.8 95.2 %all-to-all-start.2 = ((f32[32,2,2,8,1024]{4,3,2,1,0:T(8,128)}), f32[32,2,2,8,1024]{4,3,2,1,0:T(8,128)}, u32[]{:S(2)}, u32[]{:S(2)}) async-start(f32[32,2,2,8,1024]{4,3,2,1,0:T(8,128)} %copy-done), calls=%async_computation.2 | async-start | bytes 8388608 | tf_op jit(solution)/shard_map/all_to_all | solution.py:394
  50.7 1.2 copy-start.9
  51.9 1.0 copy-start.13
  53.0 2.8 copy-start.16
  55.8 1.0 copy-start.17
  63.8 1.3 copy-start.6
  65.1 78.8 %copy-start.15 = (f32[2,2,32,128]{3,2,1,0:T(8,128)S(1)}, f32[2,2,32,128]{3,2,1,0:T(8,128)}, u32[]{:S(2)}) copy-start(f32[2,2,32,128]{3,2,1,0:T(8,128)} %constant.62.clone.twist) | copy-start | bytes 196612
  138.0 54.3 %all-to-all-start.1 = ((f32[32,4,2,2,8,128]{5,4,3,2,1,0:T(8,128)}), f32[32,4,2,2,8,128]{5,4,3,2,1,0:T(8,128)}, u32[]{:S(2)}, u32[]{:S(2)}) async-start(f32[32,4,2,2,8,128]{5,4,3,2,1,0:T(8,128)} %copy-done.6), calls=%async_computation.1 | async-start | bytes 4194304 | tf_op jit(solution)/shard_map/all_to_all | solution.py:394
  144.0 1.4 copy-start.7
  150.6 1.9 copy-start.3
  192.3 2.2 copy-start.4
  194.4 1.4 copy-start.8
  205.4 97.0 %copy-start.10 = (bf16[256,1536]{1,0:T(8,128)(2,1)S(1)}, bf16[256,1536]{1,0:T(8,128)(2,1)}, u32[]{:S(2)}) copy-start(bf16[256,1536]{1,0:T(8,128)(2,1)} %constant.64.clone.table) | copy-start | bytes 2359300
